TPU v7x, 512 devices: a whole 4x8x8 slice. The times are simulated.
512 devices in a mesh: seq: 32 (over y, z_lo), tp: 16 (over z_hi, x, core).
Axes of the slice: x: 4, y: 8, z: 8 (z_hi: 2, z_lo: 4; z = z_hi * 4 + z_lo), core: 2. Of those that a mesh axis runs over, the one named last changes fastest.
Arguments:
- query_two: bfloat16 [4096, 4096], P('seq', 'tp'), may hold values from -128 to 128
- key_two: bfloat16 [4096, 4096], P('seq', 'tp'), may hold values from -6 to 6
- value_two: bfloat16 [4096, 4096], P('seq', 'tp'), may hold values from -6 to 6
- cotangent_two: bfloat16 [4096, 5120], P('seq', 'tp'), may hold values from -6 to 6
- kept_two: int32 [4096], P('seq'), may hold values from -1 to 16383, as said below
- query_three: bfloat16 [2048, 4096], P('seq', 'tp'), may hold values from -128 to 128
- key_three: bfloat16 [2048, 4096], P('seq', 'tp'), may hold values from -6 to 6
- value_three: bfloat16 [2048, 4096], P('seq', 'tp'), may hold values from -6 to 6
- cotangent_three: bfloat16 [2048, 5120], P('seq', 'tp'), may hold values from -6 to 6
- kept_three: int32 [2048], P('seq'), may hold values from -1 to 16383, as said below
- out_weight: bfloat16 [4096, 5120], P('tp'), may hold values from -0.09375 to 0.09375
Outputs:
- grad_query_two: bfloat16 [4096, 4096], P('seq', 'tp')
- grad_key_two: bfloat16 [4096, 4096], P('seq', 'tp')
- grad_value_two: bfloat16 [4096, 4096], P('seq', 'tp')
- grad_query_three: bfloat16 [2048, 4096], P('seq', 'tp')
- grad_key_three: bfloat16 [2048, 4096], P('seq', 'tp')
- grad_value_three: bfloat16 [2048, 4096], P('seq', 'tp')
Inputs may be any that keep to these rules, and one draw needn't show every extreme that they name: `kept_two`: index k of seq holds slots k * 128 to (k+1) * 128 - 1: kept positions from k * 512 to (k+1) * 512 - 1 in increasing order, then -1 for empty slots; 64 or more live slots on each index, all 128 live on some index. `kept_three`: positions also kept at depth two, in blocks of 128 slots; block k takes its positions from those of seq indices 2 * k and 2 * k + 1, increasing, live slots first and -1 after; some block is full.
All inputs are finite; a program needn't handle non-finite values.
Results may differ from a plain program's by a relative error of at most 0.01.
Values may be sent and summed in bfloat16 or wider, within the bound.
A program may use at most 64 MiB of HBM per device.

v0:
```python
import math

import jax
import jax.numpy as jnp
from jax import lax
from jax.sharding import PartitionSpec as P

HEAD_DIM = 128


NEG = -1e30
score_block = 512


def heads_view(matrix):
    return matrix.reshape(matrix.shape[0], matrix.shape[1] // HEAD_DIM, HEAD_DIM)


def project(cotangent, out_weight):
    return jnp.einsum(
        "rd,cd->rc", cotangent, out_weight, preferred_element_type=jnp.float32
    ).astype(jnp.bfloat16)


def masked_scores(query_block, key_block, query_pos, key_pos):
    scores = jnp.einsum(
        "rhe,che->hrc", query_block, key_block, preferred_element_type=jnp.float32
    ) * (1.0 / math.sqrt(HEAD_DIM))
    allowed = (
        (query_pos[:, None] >= 0)
        & (key_pos[None, :] >= 0)
        & (key_pos[None, :] <= query_pos[:, None])
    )
    return (jnp.where(allowed[None], scores, NEG), allowed[None])


def finish_stats(maximum, row_total, numerator, positions):
    live_rows = (positions >= 0)[None, :]
    safe_total = jnp.where(live_rows, row_total, 1.0)
    log_sum = jnp.where(live_rows, maximum + jnp.log(safe_total), 0.0)
    return (log_sum, numerator / safe_total)


def query_stats(query_heads, outer_heads, query_pos, key_heads, value_heads, key_pos, block_total):
    head_count = query_heads.shape[1]
    row_count = query_heads.shape[0]

    def advance(block_id, carried):
        offset = block_id * score_block
        key_block = lax.dynamic_slice_in_dim(key_heads, offset, score_block, 0)
        value_block = lax.dynamic_slice_in_dim(value_heads, offset, score_block, 0)
        pos_block = lax.dynamic_slice_in_dim(key_pos, offset, score_block, 0)
        scores, allowed = masked_scores(query_heads, key_block, query_pos, pos_block)
        grad_probs = jnp.einsum(
            "rhe,che->hrc", outer_heads, value_block, preferred_element_type=jnp.float32
        )
        new_max = jnp.maximum(carried[0], scores.max(axis=2))
        rescale = jnp.exp(carried[0] - new_max)
        weights = jnp.where(allowed, jnp.exp(scores - new_max[:, :, None]), 0.0)
        return (
            new_max,
            carried[1] * rescale + weights.sum(axis=2),
            carried[2] * rescale + (weights * grad_probs).sum(axis=2),
        )

    zeros = jnp.zeros((head_count, row_count), jnp.float32)
    start_state = (jnp.full((head_count, row_count), NEG, jnp.float32), zeros, zeros)
    final = lax.fori_loop(0, block_total, advance, start_state)
    return finish_stats(final[0], final[1], final[2], query_pos)


def query_grads(
    query_heads,
    outer_heads,
    query_pos,
    key_heads,
    value_heads,
    key_pos,
    log_sum,
    delta_sum,
    block_total,
):
    row_count = query_heads.shape[0]

    def advance(block_id, running):
        offset = block_id * score_block
        key_block = lax.dynamic_slice_in_dim(key_heads, offset, score_block, 0)
        value_block = lax.dynamic_slice_in_dim(value_heads, offset, score_block, 0)
        pos_block = lax.dynamic_slice_in_dim(key_pos, offset, score_block, 0)
        scores, allowed = masked_scores(query_heads, key_block, query_pos, pos_block)
        probability = jnp.where(allowed, jnp.exp(scores - log_sum[:, :, None]), 0.0)
        grad_probs = jnp.einsum(
            "rhe,che->hrc", outer_heads, value_block, preferred_element_type=jnp.float32
        )
        grad_scores = probability * (grad_probs - delta_sum[:, :, None])
        return running + jnp.einsum(
            "hrc,che->rhe",
            grad_scores.astype(jnp.bfloat16),
            key_block,
            preferred_element_type=jnp.float32,
        )

    summed = lax.fori_loop(0, block_total, advance, jnp.zeros(query_heads.shape, jnp.float32))
    return (summed * (1.0 / math.sqrt(HEAD_DIM))).astype(jnp.bfloat16).reshape(row_count, -1)


def key_grads(
    key_heads,
    value_heads,
    key_pos,
    query_all,
    outer_all,
    query_pos_all,
    log_sum_all,
    delta_all,
    first_block,
    block_total,
):
    row_count = key_heads.shape[0]

    def advance(block_id, running):
        offset = (first_block + block_id) * score_block
        query_block = lax.dynamic_slice_in_dim(query_all, offset, score_block, 0)
        outer_block = lax.dynamic_slice_in_dim(outer_all, offset, score_block, 0)
        pos_block = lax.dynamic_slice_in_dim(query_pos_all, offset, score_block, 0)
        lse_block = lax.dynamic_slice_in_dim(log_sum_all, offset, score_block, 1)
        delta_block = lax.dynamic_slice_in_dim(delta_all, offset, score_block, 1)
        scores, allowed = masked_scores(query_block, key_heads, pos_block, key_pos)
        probability = jnp.where(allowed, jnp.exp(scores - lse_block[:, :, None]), 0.0)
        grad_probs = jnp.einsum(
            "rhe,che->hrc", outer_block, value_heads, preferred_element_type=jnp.float32
        )
        grad_scores = probability * (grad_probs - delta_block[:, :, None])
        key_sum = running[0] + jnp.einsum(
            "hrc,rhe->che",
            grad_scores.astype(jnp.bfloat16),
            query_block,
            preferred_element_type=jnp.float32,
        )
        value_sum = running[1] + jnp.einsum(
            "hrc,rhe->che",
            probability.astype(jnp.bfloat16),
            outer_block,
            preferred_element_type=jnp.float32,
        )
        return (key_sum, value_sum)

    start_state = (jnp.zeros(key_heads.shape, jnp.float32), jnp.zeros(key_heads.shape, jnp.float32))
    sums = lax.fori_loop(0, block_total, advance, start_state)
    grad_key = (sums[0] * (1.0 / math.sqrt(HEAD_DIM))).astype(jnp.bfloat16).reshape(row_count, -1)
    grad_value = sums[1].astype(jnp.bfloat16).reshape(row_count, -1)
    return (grad_key, grad_value)


def on_device(
    query_two,
    key_two,
    value_two,
    cotangent_two,
    kept_two,
    query_three,
    key_three,
    value_three,
    cotangent_three,
    kept_three,
    out_weight,
):
    features_two, features_three = (
        lax.all_gather(cotangent_two, "tp", axis=1, tiled=True),
        lax.all_gather(cotangent_three, "tp", axis=1, tiled=True),
    )
    outer_two = project(features_two, out_weight)
    outer_three = project(features_three, out_weight)
    positions_two, positions_three = (
        lax.all_gather(kept_two, "seq", axis=0, tiled=True),
        lax.all_gather(kept_three, "seq", axis=0, tiled=True),
    )
    keys_all_two, values_all_two, keys_all_three, values_all_three = (
        lax.all_gather(key_two, "seq", axis=0, tiled=True),
        lax.all_gather(value_two, "seq", axis=0, tiled=True),
        lax.all_gather(key_three, "seq", axis=0, tiled=True),
        lax.all_gather(value_three, "seq", axis=0, tiled=True),
    )
    local_sets = [
        (
            query_two,
            outer_two,
            kept_two,
            key_two,
            value_two,
            positions_two,
            keys_all_two,
            values_all_two,
        ),
        (
            query_three,
            outer_three,
            kept_three,
            key_three,
            value_three,
            positions_three,
            keys_all_three,
            values_all_three,
        ),
    ]
    plans = []
    for member in local_sets:
        row_count = member[0].shape[0]
        block_all = member[6].shape[0] // score_block
        first_block = 0
        plans.append((row_count, block_all, first_block, block_all - first_block))
    own_stats = []
    for member, plan in zip(local_sets, plans):
        own_stats.append(
            query_stats(
                heads_view(member[0]),
                heads_view(member[1]),
                member[2],
                heads_view(member[6]),
                heads_view(member[7]),
                member[5],
                plan[1],
            )
        )
    query_all_two, outer_all_two, query_all_three, outer_all_three = (
        lax.all_gather(query_two, "seq", axis=0, tiled=True),
        lax.all_gather(outer_two, "seq", axis=0, tiled=True),
        lax.all_gather(query_three, "seq", axis=0, tiled=True),
        lax.all_gather(outer_three, "seq", axis=0, tiled=True),
    )
    gathered_rows = [(query_all_two, outer_all_two), (query_all_three, outer_all_three)]
    lse_all_two, delta_all_two, lse_all_three, delta_all_three = (
        lax.all_gather(own_stats[0][0], "seq", axis=1, tiled=True),
        lax.all_gather(own_stats[0][1], "seq", axis=1, tiled=True),
        lax.all_gather(own_stats[1][0], "seq", axis=1, tiled=True),
        lax.all_gather(own_stats[1][1], "seq", axis=1, tiled=True),
    )
    all_stats = [(lse_all_two, delta_all_two), (lse_all_three, delta_all_three)]
    results = []
    for member, plan, rows_pair, stats_pair, own_pair in zip(
        local_sets, plans, gathered_rows, all_stats, own_stats
    ):
        grad_query = query_grads(
            heads_view(member[0]),
            heads_view(member[1]),
            member[2],
            heads_view(member[6]),
            heads_view(member[7]),
            member[5],
            own_pair[0],
            own_pair[1],
            plan[1],
        )
        grad_key, grad_value = key_grads(
            heads_view(member[3]),
            heads_view(member[4]),
            member[2],
            heads_view(rows_pair[0]),
            heads_view(rows_pair[1]),
            member[5],
            stats_pair[0],
            stats_pair[1],
            plan[2],
            plan[3],
        )
        results.append((grad_query, grad_key, grad_value))
    return (
        results[0][0],
        results[0][1],
        results[0][2],
        results[1][0],
        results[1][1],
        results[1][2],
    )


def solution(mesh):
    in_specs = (
        P("seq", "tp"),
        P("seq", "tp"),
        P("seq", "tp"),
        P("seq", "tp"),
        P("seq"),
        P("seq", "tp"),
        P("seq", "tp"),
        P("seq", "tp"),
        P("seq", "tp"),
        P("seq"),
        P("tp", None),
    )
    out_specs = (
        P("seq", "tp"),
        P("seq", "tp"),
        P("seq", "tp"),
        P("seq", "tp"),
        P("seq", "tp"),
        P("seq", "tp"),
    )
    return jax.shard_map(
        on_device, mesh=mesh, in_specs=in_specs, out_specs=out_specs, check_vma=False
    )
```

profile of v0, /device:TPU:1, one launch (start us, length us, event | category | flops | bytes accessed | tf_op | source)
XLA Modules:
  0.0 1309.6 jit_solution(1582730033879494838)
XLA Ops:
  10.0 38.8 %all-gather.1 = bf16[16,320,64]{1,2,0:T(8,128)(2,1)S(1)} all-gather(bf16[1,320,64]{1,2,0:T(8,128)(2,1)} %bitcast.238), channel_id=1, replica_groups=mesh['seq'=32,'tp'=16] {'tp'}, dimensions={0}, use_global_device_ids=true | all-gather | bytes 696320 | tf_op jit(solution)/shard_map/all_gather | solution.py:170
  49.3 1.5 reshape.512
  50.8 2.7 convolution_convert_fusion.1
  55.2 25.4 %all-gather.18.cloned.1.call-done = bf16[128,5120]{0,1:T(8,128)(2,1)} async-done(((bf16[128,320]{0,1:T(8,128)(2,1)}), bf16[128,5120]{0,1:T(8,128)(2,1)}) %all-gather.18.cloned.1.call-update) | async-done | bytes 1310736 | tf_op jit(solution)/shard_map/all_gather | solution.py:169
  80.6 3.0 convolution_convert_fusion
  86.4 65.9 %all-gather = s32[32,1,128]{2,1,0:T(1,128)} all-gather(s32[1,1,128]{2,1,0:T(1,128)S(1)} %bitcast.236), channel_id=1, replica_groups=mesh['seq'=32,'tp'=16] {'seq'}, dimensions={0}, use_global_device_ids=true | all-gather | bytes 16896 | tf_op jit(solution)/shard_map/all_gather | solution.py:175
  152.3 1.6 copy.151
  158.8 10.5 all-reduce
  169.2 40.5 %all-gather.24.cloned.1.call-done = bf16[2048,256]{1,0:T(8,128)(2,1)} async-done(((bf16[64,256]{1,0:T(8,128)(2,1)}), bf16[2048,256]{1,0:T(8,128)(2,1)}) %all-gather.24.cloned.1.call-update) | async-done | bytes 1048592 | tf_op jit(solution)/shard_map/all_gather | solution.py:181
  209.7 2.3 copy.164
  212.0 2.3 copy.171
  214.3 150.2 %all-gather.26.cloned.1.call-done = bf16[2048,256]{1,0:T(8,128)(2,1)} async-done(((bf16[64,256]{1,0:T(8,128)(2,1)}), bf16[2048,256]{1,0:T(8,128)(2,1)}) %all-gather.26.cloned.1.call-update) | async-done | bytes 1048592 | tf_op jit(solution)/shard_map/all_gather | solution.py:182
  364.5 2.3 copy.165
  366.8 2.3 copy.169
  369.1 17.0 %while.99 = (s32[]{:T(128)}, f32[2,64]{1,0:T(2,128)S(1)}, f32[2,64]{1,0:T(2,128)S(1)}, f32[2,64]{1,0:T(2,128)S(1)}, s32[64]{0:T(128)}, /*index=5*/s32[2048]{0:T(...) while((s32[]{:T(128)}, f32[2,64]{1,0:T(2,128)S(1)}, ...), condition=%wide.region_13.14_spmd.clone, body=%wide.region_9.0_spmd.clone.sunk | while | flops 34309572 | bytes 1524562 | solution.py:68
  386.1 16.4 %while.100 = (s32[]{:T(128)}, f32[64,2,128]{2,0,1:T(8,128)S(1)}, bf16[2048,2,128]{2,0,1:T(8,128)(2,1)}, s32[64]{0:T(128)}, s32[2048]{0:T(1024)S(1)}, /*index=5*/...) while((s32[]{:T(128)}, f32[64,2,128]{2,0,1:T(8,128)S(1)}, ...), condition=%wide.region_15.16_spmd.clone, body=%wide.region_14.15_spmd.clone.sunk | while | flops 50922052 | bytes 1583436 | solution.py:103
  388.9 1.4 fusion.217
  393.0 1.4 fusion.217
  397.1 1.4 fusion.217
  401.2 1.4 fusion.217
  403.2 64.8 %all-gather.2 = f32[32,64,2]{1,2,0:T(2,128)S(1)} all-gather(f32[1,64,2]{1,2,0:T(2,128)S(1)} %bitcast.241), channel_id=1, replica_groups=mesh['seq'=32,'tp'=16] {'seq'}, dimensions={0}, use_global_device_ids=true | all-gather | bytes 16896 | tf_op jit(solution)/shard_map/all_gather | solution.py:235
  468.7 60.5 %all-gather.3 = f32[32,64,2]{1,2,0:T(2,128)S(1)} all-gather(f32[1,64,2]{1,2,0:T(2,128)S(1)} %bitcast.237), channel_id=1, replica_groups=mesh['seq'=32,'tp'=16] {'seq'}, dimensions={0}, use_global_device_ids=true | all-gather | bytes 16896 | tf_op jit(solution)/shard_map/all_gather | solution.py:236
  529.9 2.3 copy.176
  532.1 142.3 %all-gather.30.cloned.1.call-done = bf16[2048,256]{1,0:T(8,128)(2,1)} async-done(((bf16[64,256]{1,0:T(8,128)(2,1)}), bf16[2048,256]{1,0:T(8,128)(2,1)}) %all-gather.30.cloned.1.call-update) | async-done | bytes 1048592 | tf_op jit(solution)/shard_map/all_gather | solution.py:229
  674.4 2.1 reshape.502
  676.6 24.2 %while.101 = (s32[]{:T(128)}, f32[64,2,128]{2,0,1:T(8,128)S(1)}, f32[64,2,128]{2,0,1:T(8,128)S(1)}, bf16[2048,2,128]{0,2,1:T(8,128)(2,1)}, s32[2048]{0:T(1024)S(...) while((s32[]{:T(128)}, f32[64,2,128]{2,0,1:T(8,128)S(1)}, ...), condition=%wide.region_17.18_spmd.clone, body=%wide.region_16.17_spmd.clone.sunk | while | flops 67797568 | bytes 2785122 | solution.py:149
  681.1 1.3 fusion.226
  687.2 1.3 fusion.226
  693.2 1.3 fusion.226
  699.3 1.3 fusion.226
  702.9 110.5 %all-gather.14.cloned.1.call-done = bf16[4096,256]{0,1:T(8,128)(2,1)} async-done(((bf16[128,256]{0,1:T(8,128)(2,1)}), bf16[4096,256]{0,1:T(8,128)(2,1)}) %all-gather.14.cloned.1.call-update) | async-done | bytes 2097168 | tf_op jit(solution)/shard_map/all_gather | solution.py:179
  813.5 4.1 copy.150
  817.6 131.4 %all-gather.16.cloned.1.call-done = bf16[4096,256]{0,1:T(8,128)(2,1)} async-done(((bf16[128,256]{0,1:T(8,128)(2,1)}), bf16[4096,256]{0,1:T(8,128)(2,1)}) %all-gather.16.cloned.1.call-update) | async-done | bytes 2097168 | tf_op jit(solution)/shard_map/all_gather | solution.py:180
  949.0 4.1 copy.148
  953.1 37.8 %while.96 = (s32[]{:T(128)}, f32[2,128]{1,0:T(2,128)S(1)}, f32[2,128]{1,0:T(2,128)S(1)}, f32[2,128]{1,0:T(2,128)}, s32[128]{0:T(128)S(1)}, /*index=5*/s32[4096]{...) while((s32[]{:T(128)}, f32[2,128]{1,0:T(2,128)S(1)}, ...), condition=%wide.region_4.5_spmd.clone, body=%wide.region_0.4_spmd.clone.sunk | while | flops 68618624 | bytes 2517458 | solution.py:68
  992.2 30.0 %while.97 = (s32[]{:T(128)}, f32[128,2,128]{0,2,1:T(8,128)S(1)}, bf16[4096,2,128]{2,0,1:T(8,128)(2,1)}, s32[128]{0:T(128)S(1)}, s32[4096]{0:T(1024)}, /*index=5*...) while((s32[]{:T(128)}, f32[128,2,128]{0,2,1:T(8,128)S(1)}, ...), condition=%wide.region_6.7_spmd.clone, body=%wide.region_5.6_spmd.clone.sunk | while | flops 101843584 | bytes 2371532 | solution.py:103
  994.4 1.5 fusion.192
  998.1 1.5 fusion.192
  1001.9 1.5 fusion.192
  1005.6 1.5 fusion.192
  1009.4 1.5 fusion.192
  1013.1 1.5 fusion.192
  1016.9 1.5 fusion.192
  1020.6 1.5 fusion.192
  1022.9 67.7 %all_gather.53 = f32[2,4096]{1,0:T(2,128)} all-gather(f32[2,128]{1,0:T(2,128)} %get-tuple-element.2440), channel_id=1, replica_groups=mesh['seq'=32,'tp'=16] {'seq'}, dimensions={1}, use_global_device_ids=true | all-gather | bytes 33792 | tf_op jit(solution)/shard_map/all_gather | solution.py:233
  1090.6 63.3 %all_gather.55 = f32[2,4096]{1,0:T(2,128)} all-gather(f32[2,128]{1,0:T(2,128)S(1)} %get-tuple-element.2439), channel_id=1, replica_groups=mesh['seq'=32,'tp'=16] {'seq'}, dimensions={1}, use_global_device_ids=true | all-gather | bytes 33792 | tf_op jit(solution)/shard_map/all_gather | solution.py:234
  1154.0 4.0 reshape.491
  1158.0 84.5 %all-gather.20.cloned.1.call-done = bf16[4096,256]{0,1:T(8,128)(2,1)} async-done(((bf16[128,256]{0,1:T(8,128)(2,1)}), bf16[4096,256]{0,1:T(8,128)(2,1)}) %all-gather.20.cloned.1.call-update) | async-done | bytes 2097168 | tf_op jit(solution)/shard_map/all_gather | solution.py:226
  1242.5 58.1 %while.98 = (s32[]{:T(128)}, f32[128,2,128]{0,2,1:T(8,128)S(1)}, f32[128,2,128]{0,2,1:T(8,128)}, bf16[4096,2,128]{0,2,1:T(8,128)(2,1)}, s32[4096]{0:T(1024)}, /*...) while((s32[]{:T(128)}, f32[128,2,128]{0,2,1:T(8,128)S(1)}, ...), condition=%wide.region_8.9_spmd.clone, body=%wide.region_7.8_spmd.clone.sunk | while | flops 135594624 | bytes 3965410 | solution.py:149
  1246.6 1.4 fusion.201
  1253.1 1.4 fusion.201
  1254.5 1.9 fusion.202
  1260.5 1.4 fusion.201
  1261.9 1.9 fusion.202
  1267.8 1.4 fusion.201
  1269.3 1.9 fusion.202
  1275.2 1.4 fusion.201
  1276.6 1.9 fusion.202
  1282.6 1.4 fusion.201
  1284.0 1.9 fusion.202
  1290.0 1.4 fusion.201
  1291.4 1.9 fusion.202
  1297.4 1.4 fusion.201
  1298.8 1.9 fusion.202
  (327 shorter events, 155.7 us)
Async XLA Ops:
  7.2 43.6 %copy-start = (bf16[256,5120]{1,0:T(8,128)(2,1)S(1)}, bf16[256,5120]{1,0:T(8,128)(2,1)}, u32[]{:S(2)}) copy-start(bf16[256,5120]{1,0:T(8,128)(2,1)} %param.33) | copy-start | bytes 7864324
  7.2 73.4 %all-gather.18.cloned.1.call-start = ((), (), s32[]{:S(2)}) async-start(), calls=%async_computation.2 | async-start | bytes 1392640 | tf_op jit(solution)/shard_map/all_gather | solution.py:169
  7.9 201.8 %all-gather.24.cloned.1.call-start = ((), (), s32[]{:S(2)}) async-start(), calls=%async_computation.5 | async-start | bytes 1081344 | tf_op jit(solution)/shard_map/all_gather | solution.py:181
  8.7 355.9 %all-gather.26.cloned.1.call-start = ((), (), s32[]{:S(2)}) async-start(), calls=%async_computation.6 | async-start | bytes 1081344 | tf_op jit(solution)/shard_map/all_gather | solution.py:182
  9.4 520.5 %all-gather.28.cloned.1.call-start = ((), (), s32[]{:S(2)}) async-start(), calls=%async_computation.7 | async-start | bytes 1081344 | tf_op jit(solution)/shard_map/all_gather | solution.py:228
  10.0 664.5 %all-gather.30.cloned.1.call-start = ((), (), s32[]{:S(2)}) async-start(), calls=%async_computation.8 | async-start | bytes 1081344 | tf_op jit(solution)/shard_map/all_gather | solution.py:229
  49.3 4.2 copy-start.9
  50.8 3.6 copy-start.10
  53.4 760.0 %all-gather.14.cloned.1.call-start = ((), (), s32[]{:S(2)}) async-start(), calls=%async_computation | async-start | bytes 2162688 | tf_op jit(solution)/shard_map/all_gather | solution.py:179
  54.3 894.7 %all-gather.16.cloned.1.call-start = ((), (), s32[]{:S(2)}) async-start(), calls=%async_computation.1 | async-start | bytes 2162688 | tf_op jit(solution)/shard_map/all_gather | solution.py:180
  55.0 28.6 %copy-start.11 = (bf16[128,256]{1,0:T(8,128)(2,1)S(1)}, bf16[128,256]{1,0:T(8,128)(2,1)}, u32[]{:S(2)}) copy-start(bf16[128,256]{1,0:T(8,128)(2,1)} %param.23) | copy-start | bytes 196612
  55.1 29.4 %copy-start.7 = (bf16[64,256]{1,0:T(8,128)(2,1)S(1)}, bf16[64,256]{1,0:T(8,128)(2,1)}, u32[]{:S(2)}) copy-start(bf16[64,256]{1,0:T(8,128)(2,1)} %param.28) | copy-start | bytes 98308
  55.1 29.5 %copy-start.3 = (bf16[64,256]{1,0:T(8,128)(2,1)S(1)}, bf16[64,256]{1,0:T(8,128)(2,1)}, u32[]{:S(2)}) copy-start(bf16[64,256]{1,0:T(8,128)(2,1)} %convolution_convert_fusion.1) | copy-start | bytes 98308
  55.1 29.5 %copy-start.5 = (bf16[64,256]{1,0:T(8,128)(2,1)S(1)}, bf16[64,256]{1,0:T(8,128)(2,1)}, u32[]{:S(2)}) copy-start(bf16[64,256]{1,0:T(8,128)(2,1)} %param.29) | copy-start | bytes 98308
  55.1 30.1 %copy-start.6 = (bf16[64,256]{1,0:T(8,128)(2,1)S(1)}, bf16[64,256]{1,0:T(8,128)(2,1)}, u32[]{:S(2)}) copy-start(bf16[64,256]{1,0:T(8,128)(2,1)} %param.30) | copy-start | bytes 98308
  55.1 30.7 %copy-start.4 = (s32[128]{0:T(128)S(1)}, s32[128]{0:T(128)}, u32[]{:S(2)}) copy-start(s32[128]{0:T(128)} %param.27) | copy-start | bytes 1540
  55.1 98.7 %copy-start.1 = (bf16[128,256]{0,1:T(8,128)(2,1)S(1)}, bf16[128,256]{0,1:T(8,128)(2,1)}, u32[]{:S(2)}) copy-start(bf16[128,256]{0,1:T(8,128)(2,1)} %copy.143) | copy-start | bytes 196612
  55.1 99.4 %copy-start.2 = (bf16[128,256]{0,1:T(8,128)(2,1)S(1)}, bf16[128,256]{0,1:T(8,128)(2,1)}, u32[]{:S(2)}) copy-start(bf16[128,256]{0,1:T(8,128)(2,1)} %copy.145) | copy-start | bytes 196612
  55.2 1098.8 %all-gather.22.cloned.1.call-start = ((), (), s32[]{:S(2)}) async-start(), calls=%async_computation.4 | async-start | bytes 2162688 | tf_op jit(solution)/shard_map/all_gather | solution.py:227
  83.6 1158.9 %all-gather.20.cloned.1.call-start = ((), (), s32[]{:S(2)}) async-start(), calls=%async_computation.3 | async-start | bytes 2162688 | tf_op jit(solution)/shard_map/all_gather | solution.py:226
  214.3 154.8 %copy-start.13 = (f32[2,64]{1,0:T(2,128)S(1)}, f32[2,64]{1,0:T(2,128)}, u32[]{:S(2)}) copy-start(f32[2,64]{1,0:T(2,128)} %custom-call.7) | copy-start | bytes 1540
  214.3 154.8 %copy-start.14 = (f32[2,64]{1,0:T(2,128)S(1)}, f32[2,64]{1,0:T(2,128)}, u32[]{:S(2)}) copy-start(f32[2,64]{1,0:T(2,128)} %custom-call.8) | copy-start | bytes 1540
  949.0 4.1 copy-start.8
  949.0 4.1 copy-start.12
Sparse Core Ops, SparseCore 0:
  11.3 69.2 all-gather.17
  82.7 126.9 all-gather.23
  211.8 152.6 all-gather.25
  366.5 152.7 all-gather.27
  521.7 152.6 all-gather.29
  676.9 136.5 all-gather.13
  815.5 133.4 all-gather.15
  951.1 152.9 all-gather.21
  1106.7 135.7 all-gather.19
where the time goes:
time: 1330 us; the launch traced here: 1310 us
  waiting for transfers between devices  688 us (52%)
  blocking collectives  371 us (28%)
  matrix products  113 us (8%)
  local copies, waits for them, and re-layouts  63.9 us (5%)
  other arithmetic  56.5 us (4%)
  between operations  14.8 us (1%)
    all_gather x1, waiting for transfers between devices, on_device(): lax.all_gather(value_three, 'seq', axis=0, tiled=True)  150 us
    all_gather x1, waiting for transfers between devices, on_device(): lax.all_gather(outer_three, 'seq', axis=0, tiled=True)  142 us
    all_gather x1, waiting for transfers between devices, on_device(): lax.all_gather(value_two, 'seq', axis=0, tiled=True)  131 us
    all_gather x1, waiting for transfers between devices, on_device(): lax.all_gather(key_two, 'seq', axis=0, tiled=True)  111 us
    all_gather x1, waiting for transfers between devices, on_device(): lax.all_gather(query_two, 'seq', axis=0, tiled=True)  84.5 us
    all_gather x1, blocking collectives, on_device(): lax.all_gather(own_stats[0][0], 'seq', axis=1, tiled=True)  67.7 us
    all_gather x1, blocking collectives, on_device(): lax.all_gather(kept_two, 'seq', axis=0, tiled=True)  65.9 us
    all_gather x1, blocking collectives, on_device(): lax.all_gather(own_stats[1][0], 'seq', axis=1, tiled=True)  64.8 us
  transfers between devices with their start and end apart: 9, of which 7 were waited for; matrix products, arithmetic and copies ran while one was open for 13% of the time, Pallas kernels for 0%

commit v1 on v0

v1 whole, which is shorter than its diff:
```python
import functools
import math

import jax
import jax.numpy as jnp
from jax import lax
from jax.experimental import pallas as pl
from jax.experimental.pallas import tpu as pltpu
from jax.sharding import PartitionSpec as P

MESH = pl.DeviceIdType.MESH
F32, BF16 = jnp.float32, jnp.bfloat16
HEAD = 128
R2, R3 = 128, 64
RT = R2 + R3
FEAT = 320
NEG = -1e30
SCALE = 1.0 / math.sqrt(HEAD)
SLOT = 2 * RT + 16
GRAD = 2 * RT


def dot_nt(a, b):
    return lax.dot_general(a, b, (((1,), (1,)), ((), ())), preferred_element_type=F32)


def dot_nn(a, b):
    return lax.dot_general(a, b, (((1,), (0,)), ((), ())), preferred_element_type=F32)


def dot_tn(a, b):
    return lax.dot_general(a, b, (((0,), (0,)), ((), ())), preferred_element_type=F32)


def device(y, z, zh, x, c):
    return (y * 4 + z, (zh * 4 + x) * 2 + c)


def body(
    kept2, kept3, q2, k2, v2, cot2, q3, k3, v3, cot3, weight,
    dq2, dk2, dv2, dq3, dk3, dv3,
    cot, wv, kv, qb2, qb3, ob2, ob3, bias, ost, acc2, acc3, st2, st3,
    stat, stat_out, stat_in, rb, sb, tmp, dqt2, dqt3, dqx_out, dqx_in, dq_out, dq_in, back_out, back_in,
    ssem, lsem, cot_z, cot_x, cot_s, kvin, qin, oin, ring, red, ring_s, red_s, xsem, backsem, dqsem,
):
    s, t = lax.axis_index("seq"), lax.axis_index("tp")
    y, z = lax.div(s, 4), lax.rem(s, 4)
    zh, x, c = lax.div(t, 8), lax.rem(lax.div(t, 2), 4), lax.rem(t, 2)
    zhalf, zpar = lax.div(z, 2), lax.rem(z, 2)

    sent = []

    def send(src, dst, sem, to, when=None):
        copy = pltpu.make_async_remote_copy(
            src_ref=src, dst_ref=dst, send_sem=ssem.at[len(sent)], recv_sem=sem,
            device_id=to, device_id_type=MESH,
        )
        if when is None:
            copy.start()
        else:
            pl.when(when)(copy.start)
        sent.append((copy, when))

    def keep(src, dst, sem, when=None):
        copy = pltpu.make_async_copy(src, dst, sem)
        if when is None:
            copy.start()
        else:
            pl.when(when)(copy.start)

    def arrive(ref, sem):
        pltpu.make_async_copy(ref, ref, sem).wait()

    sibling = device(y, z, zh, x, 1 - c)
    y_up, y_down = lax.rem(y + 1, 8), lax.rem(y + 7, 8)

    barrier = pltpu.get_barrier_semaphore()
    peers = [device(y_up, z, zh, x, c), device(y_down, z, zh, x, c), device(y, z, 1 - zh, x, c), sibling]
    for dx in (1, 2, 3):
        peers.append(device(y, z, zh, lax.rem(x + dx, 4), c))
        for cc in (0, 1):
            peers.append(device(y, lax.rem(z + dx, 4), zh, x, cc))
    for peer in peers:
        pl.semaphore_signal(barrier, inc=1, device_id=peer, device_id_type=MESH)
    keep(cot2, cot.at[zh, x, c, 0:R2], lsem.at[0])
    keep(cot3, cot.at[zh, x, c, R2:RT], lsem.at[1])
    keep(weight, wv, lsem.at[2])
    rows = lax.broadcasted_iota(jnp.int32, (16, HEAD), 0)
    live2 = jnp.where(kept2[...] >= 0, 0.0, NEG)
    live3 = jnp.where(kept3[...] >= 0, 0.0, NEG)
    bias_value = jnp.where(rows == 0, live2, jnp.where(rows == 1, live3, 0.0))
    bias[...] = bias_value.astype(BF16)
    stat[...] = jnp.where(lax.broadcasted_iota(jnp.int32, stat.shape, 0) == 0, NEG, 0.0)
    acc2[...] = jnp.zeros_like(acc2)
    acc3[...] = jnp.zeros_like(acc3)
    dqt2[...] = jnp.zeros_like(dqt2)
    dqt3[...] = jnp.zeros_like(dqt3)
    pl.semaphore_wait(barrier, len(peers))

    far = device(y, z, 1 - zh, x, c)
    mine = cot.at[zh, x, c]
    send(cot2, mine.at[0:R2], cot_z.at[0], far)
    send(cot3, mine.at[R2:RT], cot_z.at[1], far)

    for hh in (0, 1):
        cols = pl.ds(hh * HEAD, HEAD)
        here = (zhalf == c) & (zpar == hh)
        away = jnp.logical_not(here)
        to = device(y, 2 * c + hh, zh, x, zhalf)
        slot = kv.at[y, zpar]
        sem = kvin.at[zpar]
        parts = (
            (k2.at[:, cols], slot.at[0:R2]),
            (k3.at[:, cols], slot.at[R2:RT]),
            (v2.at[:, cols], slot.at[RT:RT + R2]),
            (v3.at[:, cols], slot.at[RT + R2:GRAD]),
            (bias, slot.at[GRAD:SLOT]),
        )
        for src, dst in parts:
            keep(src, dst, sem, here)
            send(src, dst, sem, to, away)

    for dx in (1, 3, 2):
        to = device(y, z, zh, lax.rem(x + dx, 4), c)
        send(cot2, mine.at[0:R2], cot_x.at[0, x], to)
        send(cot3, mine.at[R2:RT], cot_x.at[0, x], to)
    send(cot2, mine.at[0:R2], cot_s.at[zh, x], sibling)
    send(cot3, mine.at[R2:RT], cot_s.at[zh, x], sibling)

    at2 = pl.ds(pl.multiple_of(z * R2, R2), R2)
    at3 = pl.ds(pl.multiple_of(z * R3, R3), R3)

    def to_workers(hh, part2, part3, dst2, dst3, sems):
        for cc in (0, 1):
            here = (z == 2 * c + hh) & (c == cc)
            away = jnp.logical_not(here)
            to = device(y, 2 * c + hh, zh, x, cc)
            for depth, (src, dst) in enumerate(((part2, dst2.at[at2]), (part3, dst3.at[at3]))):
                keep(src, dst, sems.at[z, depth], here)
                send(src, dst, sems.at[z, depth], to, away)

    def from_sources(dst2, dst3, sems):
        for zz in range(4):
            arrive(dst2.at[zz * R2:(zz + 1) * R2], sems.at[zz, 0])
            arrive(dst3.at[zz * R3:(zz + 1) * R3], sems.at[zz, 1])

    for hh in (0, 1):
        cols = pl.ds(hh * HEAD, HEAD)
        to_workers(hh, q2.at[:, cols], q3.at[:, cols], qb2, qb3, qin)

    ring_to = (device(y_up, z, zh, x, c), device(y_down, z, zh, x, c))

    def origin(direction, step):
        return lax.rem(y + (8 - step if direction == 0 else step), 8)

    ring_sent = []

    def ring_send(direction, step, sub, at):
        slot = kv.at[at, sub]
        copy = pltpu.make_async_remote_copy(
            src_ref=slot, dst_ref=slot, send_sem=ring_s.at[direction, step, sub], recv_sem=ring.at[direction, step, sub],
            device_id=ring_to[direction], device_id_type=MESH,
        )
        copy.start()
        ring_sent.append(copy)

    def ring_step(step):
        for sub in (0, 1):
            for direction in (0, 1):
                if step == 4 and sub != direction:
                    continue
                at = origin(direction, step)
                arrive(kv.at[at, sub], ring.at[direction, step - 1, sub])
                if step < 3 or (step == 3 and sub == direction):
                    ring_send(direction, step, sub, at)

    row2 = pl.ds(0, 512)
    row3 = pl.ds(512, 256)

    def early_part(at, sub, rows_k, rows_v, queries, column, row, store, acc, base):
        scores = dot_nt(kv[at, sub, rows_k], queries[...]) * SCALE
        key_slot = lax.broadcasted_iota(jnp.int32, scores.shape, 0) + base
        query_slot = lax.broadcasted_iota(jnp.int32, scores.shape, 1)
        scores = jnp.where(key_slot <= query_slot, scores + column, NEG)
        store[at * 2 + sub] = scores
        before = stat[0:1, row]
        now = jnp.maximum(before, jnp.max(scores, axis=0, keepdims=True))
        weights = jnp.exp(scores - now)
        fade = jnp.exp(before - now)
        stat[0:1, row] = now
        stat[1:2, row] = stat[1:2, row] * fade + jnp.sum(weights, axis=0, keepdims=True)
        acc[...] = acc[...] * fade + dot_tn(kv[at, sub, rows_v], weights.astype(BF16))

    def early(at, sub):
        @pl.when(at <= y)
        def _():
            line = kv[at, sub, GRAD:SLOT].astype(F32)
            column = jnp.concatenate([line, jnp.zeros((HEAD - 16, HEAD), F32)], axis=0).T
            part = 2 * c + sub
            early_part(at, sub, pl.ds(0, R2), pl.ds(RT, R2), qb2, column[:, 0:1], row2, st2, acc2,
                       (at - y) * 512 + part * R2)
            early_part(at, sub, pl.ds(R2, R3), pl.ds(RT + R2, R3), qb3, column[0:R3, 1:2], row3, st3, acc3,
                       (at - y) * 256 + part * R3)

    def early_step(step):
        @pl.loop(0, 2 if step in (0, 4) else 4)
        def _(j):
            sub = lax.rem(j, 2)
            if step == 0:
                early(y, sub)
            elif step == 4:
                early(lax.rem(y + 4, 8), sub)
            else:
                forward = lax.div(j, 2)
                early(lax.rem(y + 8 + (2 * forward - 1) * step, 8), sub)

    arrive(kv.at[y, 0], kvin.at[0])
    arrive(kv.at[y, 1], kvin.at[1])
    for sub in (0, 1):
        for direction in (0, 1):
            ring_send(direction, 0, sub, y)

    for dx in (1, 3, 2):
        xx = lax.rem(x + dx, 4)
        arrive(cot.at[zh, xx, c], cot_x.at[0, xx])
        send(cot.at[zh, xx, c], cot.at[zh, xx, c], cot_s.at[zh, xx], sibling)
    from_sources(qb2, qb3, qin)
    early_step(0)

    other = cot.at[1 - zh, x, c]
    for piece, rows_p in enumerate((pl.ds(0, R2), pl.ds(R2, R3))):
        arrive(other.at[rows_p], cot_z.at[piece])
        for dx in (1, 3, 2):
            to = device(y, z, zh, lax.rem(x + dx, 4), c)
            send(other.at[rows_p], other.at[rows_p], cot_x.at[1, x], to)
    send(other, other, cot_s.at[1 - zh, x], sibling)

    ring_step(1)
    early_step(1)
    ring_step(2)
    early_step(2)
    for dx in (1, 3, 2):
        xx = lax.rem(x + dx, 4)
        theirs = cot.at[1 - zh, xx, c]
        arrive(theirs, cot_x.at[1, xx])
        send(theirs, theirs, cot_s.at[1 - zh, xx], sibling)
    ring_step(3)

    for zz in (0, 1):
        for xx in range(4):
            arrive(cot.at[zz, xx, 1 - c], cot_s.at[zz, xx])
    arrive(mine.at[0:R2], lsem.at[0])
    arrive(mine.at[R2:RT], lsem.at[1])
    arrive(wv, lsem.at[2])

    def project(p, total):
        zz, xx = lax.div(p, 4), lax.rem(p, 4)
        features = jnp.concatenate([cot[zz, xx, 0], cot[zz, xx, 1]], axis=1)
        return total + dot_nt(features, wv[:, pl.ds(pl.multiple_of(p * 2 * FEAT, HEAD), 2 * FEAT)])

    outer = lax.fori_loop(0, 8, project, jnp.zeros((RT, 2 * HEAD), F32))
    lines = jnp.concatenate([bias_value, jnp.zeros((HEAD - 16, HEAD), F32)], axis=0).T
    dead = jnp.concatenate([lines[:, 0:1], lines[0:R3, 1:2]], axis=0)
    outer = jnp.where(dead < 0.0, 0.0, outer).astype(BF16)
    for hh in (0, 1):
        ost[hh] = outer[:, hh * HEAD:(hh + 1) * HEAD]
        to_workers(hh, ost.at[hh, 0:R2], ost.at[hh, R2:RT], ob2, ob3, oin)

    early_step(3)
    ring_step(4)
    early_step(4)
    from_sources(ob2, ob3, oin)

    stat_out[...] = stat[...]
    stat_out[2:3, row2] = jnp.sum(ob2[...].astype(F32).T * acc2[...], axis=0, keepdims=True)
    stat_out[2:3, row3] = jnp.sum(ob3[...].astype(F32).T * acc3[...], axis=0, keepdims=True)
    send(stat_out, stat_in, xsem.at[0], sibling)
    arrive(stat_in, xsem.at[0])
    top = jnp.maximum(stat_out[0:1], stat_in[0:1])
    own_part, other_part = jnp.exp(stat_out[0:1] - top), jnp.exp(stat_in[0:1] - top)
    total = stat_out[1:2] * own_part + stat_in[1:2] * other_part
    stat[3:4] = top + jnp.log(total)
    stat[4:5] = (stat_out[2:3] * own_part + stat_in[2:3] * other_part) / total

    def late_part(at, sub, rows_k, rows_v, queries, outers, row, store, dqt):
        probability = jnp.exp(store[at * 2 + sub] - stat[3:4, row])
        grad_probs = dot_nt(kv[at, sub, rows_v], outers[...])
        grad_low = (probability * (grad_probs - stat[4:5, row])).astype(BF16)
        tmp[rows_k] = dot_nn(grad_low, queries[...]) * SCALE
        tmp[rows_v] = dot_nn(probability.astype(BF16), outers[...])
        half = grad_low.shape[1] // 2
        for h in (0, 1):
            dqt[h] += dot_tn(kv[at, sub, rows_k], grad_low[:, h * half:(h + 1) * half])

    def late(at, sub):
        @pl.when(at <= y)
        def _():
            late_part(at, sub, pl.ds(0, R2), pl.ds(RT, R2), qb2, ob2, row2, st2, dqt2)
            late_part(at, sub, pl.ds(R2, R3), pl.ds(RT + R2, R3), qb3, ob3, row3, st3, dqt3)

        @pl.when(at > y)
        def _():
            tmp[...] = jnp.zeros_like(tmp)

    def red_copy(direction, step, sub):
        return pltpu.make_async_remote_copy(
            src_ref=sb.at[direction, step, sub], dst_ref=rb.at[direction, step, sub],
            send_sem=red_s.at[direction, step, sub], recv_sem=red.at[direction, step, sub],
            device_id=ring_to[direction], device_id_type=MESH,
        )

    for step in range(4):
        for sub in (0, 1):
            for direction in (0, 1):
                if step == 0 and sub != direction:
                    continue
                ahead = 4 - step
                at = lax.rem(y + (ahead if direction == 0 else 8 - ahead), 8)
                late(at, sub)
                value = tmp[...]
                if step > 1 or (step == 1 and sub == direction):
                    arrive(rb.at[direction, step - 1, sub], red.at[direction, step - 1, sub])
                    value = value + rb[direction, step - 1, sub].astype(F32)
                sb[direction, step, sub] = value.astype(BF16)
                red_copy(direction, step, sub).start()

    own_rows = []
    for sub in (0, 1):
        late(y, sub)
        own_rows.append(tmp[...])
        back_out[sub] = tmp[...].astype(BF16)

    dqx_out[:, 0:256] = dqt2[1 - c].astype(BF16)
    dqx_out[:, 256:384] = dqt3[1 - c].astype(BF16)
    send(dqx_out, dqx_in, xsem.at[1], sibling)
    arrive(dqx_in, xsem.at[1])
    query_two = (dqt2[c] + dqx_in[:, 0:256].astype(F32)) * SCALE
    query_three = (dqt3[c] + dqx_in[:, 256:384].astype(F32)) * SCALE
    rows_two, rows_three = query_two.T.astype(BF16), query_three.T.astype(BF16)

    def to_source(sub, src, dst, sems):
        here = (z == 2 * c + sub)
        to = device(y, 2 * c + sub, zh, x, zhalf)
        away = jnp.logical_not(here & (zhalf == c))
        keep(src, dst.at[zpar], sems.at[zpar], jnp.logical_not(away))
        send(src, dst.at[zpar], sems.at[zpar], to, away)

    for sub in (0, 1):
        dq_out[sub, 0:R2] = rows_two[sub * R2:(sub + 1) * R2]
        dq_out[sub, R2:RT] = rows_three[sub * R3:(sub + 1) * R3]
        to_source(sub, dq_out.at[sub], dq_in, dqsem)

    for sub in (0, 1):
        value = own_rows[sub]
        for direction in (0, 1):
            arrive(rb.at[direction, 3, sub], red.at[direction, 3, sub])
            value = value + rb[direction, 3, sub].astype(F32)
        back_out[sub] = value.astype(BF16)
        to_source(sub, back_out.at[sub], back_in, backsem)

    for hh in (0, 1):
        cols = pl.ds(hh * HEAD, HEAD)
        arrive(dq_in.at[hh], dqsem.at[hh])
        dq2[:, cols] = dq_in[hh, 0:R2]
        dq3[:, cols] = dq_in[hh, R2:RT]
    for hh in (0, 1):
        cols = pl.ds(hh * HEAD, HEAD)
        arrive(back_in.at[hh], backsem.at[hh])
        dk2[:, cols] = back_in[hh, 0:R2]
        dk3[:, cols] = back_in[hh, R2:RT]
        dv2[:, cols] = back_in[hh, RT:RT + R2]
        dv3[:, cols] = back_in[hh, RT + R2:GRAD]

    for copy, when in sent:
        if when is None:
            copy.wait_send()
        else:
            pl.when(when)(copy.wait_send)
    for copy in ring_sent:
        copy.wait_send()
    for step in range(4):
        for sub in (0, 1):
            for direction in (0, 1):
                if step > 0 or sub == direction:
                    red_copy(direction, step, sub).wait_send()


def on_device(q2, k2, v2, cot2, kept2, q3, k3, v3, cot3, kept3, weight):
    any_spec = pl.BlockSpec(memory_space=pl.ANY)
    vmem = pl.BlockSpec(memory_space=pltpu.VMEM)
    dma = pltpu.SemaphoreType.DMA
    line2 = kept2.reshape(1, R2)
    line3 = jnp.concatenate([kept3, jnp.zeros((HEAD - R3,), kept3.dtype)]).reshape(1, HEAD)
    wide = jax.ShapeDtypeStruct((R2, 2 * HEAD), BF16)
    narrow = jax.ShapeDtypeStruct((R3, 2 * HEAD), BF16)
    return pl.pallas_call(
        body,
        out_shape=(wide, wide, wide, narrow, narrow, narrow),
        in_specs=[vmem, vmem] + [any_spec] * 9,
        out_specs=(vmem,) * 6,
        scratch_shapes=[
            pltpu.VMEM((2, 4, 2, RT, FEAT), BF16),
            pltpu.VMEM((2 * HEAD, 16 * FEAT), BF16),
            pltpu.VMEM((8, 2, SLOT, HEAD), BF16),
            pltpu.VMEM((512, HEAD), BF16),
            pltpu.VMEM((256, HEAD), BF16),
            pltpu.VMEM((512, HEAD), BF16),
            pltpu.VMEM((256, HEAD), BF16),
            pltpu.VMEM((16, HEAD), BF16),
            pltpu.VMEM((2, RT, HEAD), BF16),
            pltpu.VMEM((HEAD, 512), F32),
            pltpu.VMEM((HEAD, 256), F32),
            pltpu.VMEM((16, R2, 512), F32),
            pltpu.VMEM((16, R3, 256), F32),
            pltpu.VMEM((8, 768), F32),
            pltpu.VMEM((8, 768), F32),
            pltpu.VMEM((8, 768), F32),
            pltpu.VMEM((2, 4, 2, GRAD, HEAD), BF16),
            pltpu.VMEM((2, 4, 2, GRAD, HEAD), BF16),
            pltpu.VMEM((GRAD, HEAD), F32),
            pltpu.VMEM((2, HEAD, 256), F32),
            pltpu.VMEM((2, HEAD, 128), F32),
            pltpu.VMEM((HEAD, 384), BF16),
            pltpu.VMEM((HEAD, 384), BF16),
            pltpu.VMEM((2, RT, HEAD), BF16),
            pltpu.VMEM((2, RT, HEAD), BF16),
            pltpu.VMEM((2, GRAD, HEAD), BF16),
            pltpu.VMEM((2, GRAD, HEAD), BF16),
            dma((64,)),
            dma((3,)),
            dma((2,)),
            dma((2, 4)),
            dma((2, 4)),
            dma((2,)),
            dma((4, 2)),
            dma((4, 2)),
            dma((2, 4, 2)),
            dma((2, 4, 2)),
            dma((2, 4, 2)),
            dma((2, 4, 2)),
            dma((2,)),
            dma((2,)),
            dma((2,)),
        ],
        compiler_params=pltpu.CompilerParams(
            collective_id=0, has_side_effects=True, vmem_limit_bytes=48 * 1024 * 1024
        ),
        name="attention_backward",
    )(line2, line3, q2, k2, v2, cot2, q3, k3, v3, cot3, weight)


def solution(mesh):
    shard = P("seq", "tp")
    in_specs = (shard, shard, shard, shard, P("seq"), shard, shard, shard, shard, P("seq"), P("tp", None))
    return jax.shard_map(on_device, mesh=mesh, in_specs=in_specs, out_specs=(shard,) * 6, check_vma=False)
```

time: 1330 us -> 94.7 us (0.07); the launches traced: 1310 us -> 94.1 us
  waiting for transfers between devices: 688 us -> 0 us
  blocking collectives: 371 us -> 0 us
  matrix products: 113 us -> 0 us
  Pallas kernels: 0 us -> 80.1 us
  other arithmetic: 56.5 us -> 0 us
  local copies, waits for them, and re-layouts: 63.9 us -> 13.4 us
  between operations: 14.8 us -> 0.66 us
    all_gather x9 -> x0, waiting for transfers between devices: 685 us -> none  [the longest x1 150 us: on_device(): lax.all_gather(value_three, 'seq', axis=0, tiled=True)]
    all_gather x6 -> x0, blocking collectives: 361 us -> none  [the longest x1 67.7 us: on_device(): lax.all_gather(own_stats[0][0], 'seq', axis=1, tiled=True)]
    dot_general x86 -> x0, matrix products: 113 us -> none  [the longest x36 44.5 us: masked_scores(): jnp.einsum('rhe,che->hrc', query_block, key_block, preferred_element_type...]
    pallas_call x0 -> x1, Pallas kernels: none -> 80.1 us  [on_device(): pl.pallas_call(body, out_shape=(wide, wide, wide, narrow, narrow, narrow)...]
    ge x74 -> x0, other arithmetic: 28.3 us -> none  [the longest x36 15.4 us: masked_scores(): key_pos[None, :] >= 0]
    dynamic_slice x24 -> x0, local copies, waits for them, and re-layouts: 21.9 us -> none  [the longest x12 13.7 us: advance(): outer_block = lax.dynamic_slice_in_dim(outer_all, offset, score_block, 0)]
    and x36 -> x0, other arithmetic: 13.9 us -> none  [masked_scores(): (query_pos[:, None] >= 0) & (key_pos[None, :] >= 0)]
  transfers between devices with their start and end apart: 9 -> 0, of which waited for: 7 -> 0; matrix products, arithmetic and copies ran while one was open for 13% -> 0% of each run, Pallas kernels for 0% -> 0%
where the time goes in v1:
time: 94.7 us; the launch traced here: 94.1 us
  Pallas kernels  80.1 us (85%)
  local copies, waits for them, and re-layouts  13.4 us (14%)
    pallas_call x1, Pallas kernels, on_device(): pl.pallas_call(body, out_shape=(wide, wide, wide, narrow, narrow, narrow)...  80.1 us
    unnamed x25, local copies, waits for them, and re-layouts  12.7 us

profile of v1, /device:TPU:1, one launch (start us, length us, event | category | flops | bytes accessed | tf_op | source)
XLA Modules:
  0.0 94.1 jit_solution(5110554009829245125)
XLA Ops:
  0.6 0.7 pad_bitcast_fusion.kept3
  1.3 1.0 %copy.17.cot2 = bf16[128,320]{1,0:T(8,128)(2,1)S(1)} copy(bf16[128,320]{0,1:T(8,128)(2,1)} %param.14) | data formatting | bytes 163840 | tf_op args[3]
  2.3 0.0 copy-start
  2.3 1.7 %copy-done = bf16[256,5120]{1,0:T(8,128)(2,1)S(1)} copy-done((bf16[256,5120]{1,0:T(8,128)(2,1)S(1)}, bf16[256,5120]{1,0:T(8,128)(2,1)}, u32[]{:S(2)}) %copy-start) | copy-done | bytes 2621464
  4.0 0.0 copy-start.1
  4.0 0.8 copy-done.1
  4.9 0.0 copy-start.2
  4.9 0.8 copy-done.2
  5.7 0.0 copy-start.3
  5.7 0.8 copy-done.3
  6.6 0.0 copy-start.4
  6.6 0.8 copy-done.4
  7.4 0.0 copy-start.5
  7.4 0.8 copy-done.5
  8.1 0.0 copy-start.6
  8.1 0.8 copy-done.6
  8.9 0.0 copy-start.7
  8.9 0.8 copy-done.7
  9.6 0.0 copy-start.8
  9.6 0.7 copy-done.8
  10.3 80.1 %attention_backward.1 = (bf16[128,256]{1,0:T(8,128)(2,1)S(1)}, bf16[128,256]{1,0:T(8,128)(2,1)S(1)}, bf16[128,256]{1,0:T(8,128)(2,1)S(1)}, bf16[64,256]{1,0:T(8,...) custom-call(s32[1,128]{1,0:T(1,128)S(1)} %bitcast.3, s32[1,128]{1,0:T(1,128)S(1)} %pad_bitcast_fusion.kept3, ...), custom_call_target="tpu_custom_call" | custom-call | tf_op jit(solution)/shard_map/attention_backward/pallas_call | solution.py:396
  90.4 0.6 copy.24
  91.0 0.6 copy.25
  91.6 0.6 copy.26
  92.2 0.6 copy.27
  92.9 0.6 copy.28
  93.5 0.6 copy.29
Async XLA Ops:
  2.3 1.7 %copy-start = (bf16[256,5120]{1,0:T(8,128)(2,1)S(1)}, bf16[256,5120]{1,0:T(8,128)(2,1)}, u32[]{:S(2)}) copy-start(bf16[256,5120]{1,0:T(8,128)(2,1)} %weight.1) | copy-start | bytes 7864324
  4.0 0.8 copy-start.1
  4.9 0.8 copy-start.2
  5.7 0.8 copy-start.3
  6.6 0.8 copy-start.4
  7.4 0.8 copy-start.5
  8.1 0.8 copy-start.6
  8.9 0.8 copy-start.7
  9.6 0.7 copy-start.8

commit v2 on v1

v2 whole, which is shorter than its diff:
```python
import functools
import math

import jax
import jax.numpy as jnp
from jax import lax
from jax.experimental import pallas as pl
from jax.experimental.pallas import tpu as pltpu
from jax.sharding import PartitionSpec as P

MESH = pl.DeviceIdType.MESH
F32, BF16 = jnp.float32, jnp.bfloat16
HEAD = 128
R2, R3 = 128, 64
RT = R2 + R3
FEAT = 320
NEG = -1e30
SCALE = 1.0 / math.sqrt(HEAD)
SCALE_TWO = SCALE * math.log2(math.e)
SLOT = 2 * RT + 16
GRAD = 2 * RT


def dot_nt(a, b):
    return lax.dot_general(a, b, (((1,), (1,)), ((), ())), preferred_element_type=F32)


def dot_nn(a, b):
    return lax.dot_general(a, b, (((1,), (0,)), ((), ())), preferred_element_type=F32)


def dot_tn(a, b):
    return lax.dot_general(a, b, (((0,), (0,)), ((), ())), preferred_element_type=F32)


def device(y, z, zh, x, c):
    return (y * 4 + z, (zh * 4 + x) * 2 + c)


def body(
    kept2, kept3, q2, k2, v2, cot2, q3, k3, v3, cot3, weight,
    dq_got, back_got,
    ct2, ct3, line2, line3, wv, kv, qb2, qb3, qt2, qt3, ob2, ob3, bias, outer2, outer3, ost2, ost3, acc2, acc3, st2, st3,
    stat, stat_out, stat_in, rb, sb, tmp, dqt2, dqt3, dqx_out, dqx_in, dq_out, dq_in, back_out, back_in,
    ssem, lsem, cot_z, cot_x, cot_s, kvin, qin, oin, ring, red, ring_s, red_s, xsem, backsem, dqsem,
):
    s, t = lax.axis_index("seq"), lax.axis_index("tp")
    y, z = lax.div(s, 4), lax.rem(s, 4)
    zh, x, c = lax.div(t, 8), lax.rem(lax.div(t, 2), 4), lax.rem(t, 2)
    zhalf, zpar = lax.div(z, 2), lax.rem(z, 2)

    sent = []

    def send(src, dst, sem, to, when=None):
        copy = pltpu.make_async_remote_copy(
            src_ref=src, dst_ref=dst, send_sem=ssem.at[len(sent)], recv_sem=sem,
            device_id=to, device_id_type=MESH,
        )
        if when is None:
            copy.start()
        else:
            pl.when(when)(copy.start)
        sent.append((copy, when))

    def keep(src, dst, sem, when=None):
        copy = pltpu.make_async_copy(src, dst, sem)
        if when is None:
            copy.start()
        else:
            pl.when(when)(copy.start)

    def arrive(ref, sem):
        pltpu.make_async_copy(ref, ref, sem).wait()

    def ct2_at(zz, xx, cc):
        return ct2.at[zz, xx, pl.ds(pl.multiple_of(cc * FEAT, 64), FEAT)]

    sibling = device(y, z, zh, x, 1 - c)
    y_up, y_down = lax.rem(y + 1, 8), lax.rem(y + 7, 8)

    barrier = pltpu.get_barrier_semaphore()
    peers = [device(y_up, z, zh, x, c), device(y_down, z, zh, x, c), device(y, z, 1 - zh, x, c), sibling]
    for dx in (1, 2, 3):
        peers.append(device(y, z, zh, lax.rem(x + dx, 4), c))
        for cc in (0, 1):
            peers.append(device(y, lax.rem(z + dx, 4), zh, x, cc))
    for peer in peers:
        pl.semaphore_signal(barrier, inc=1, device_id=peer, device_id_type=MESH)
    keep(kept2, line2, lsem.at[3])
    keep(kept3, line3, lsem.at[4])
    keep(cot2, ct2_at(zh, x, c), lsem.at[0])
    keep(cot3, ct3.at[zh, x, c], lsem.at[1])
    keep(weight, wv, lsem.at[2])
    pl.semaphore_wait(barrier, len(peers))

    def clear():
        stat[...] = jnp.where(lax.broadcasted_iota(jnp.int32, stat.shape, 0) == 0, NEG, 0.0)
        for ref in (acc2, acc3, dqt2, dqt3, outer2, outer3):
            ref[...] = jnp.zeros_like(ref)

    far = device(y, z, 1 - zh, x, c)
    mine2, mine3 = ct2_at(zh, x, c), ct3.at[zh, x, c]
    def cot_far():
        send(cot2, mine2, cot_z.at[0], far)
        send(cot3, mine3, cot_z.at[1], far)

    def make_bias():
        arrive(line2, lsem.at[3])
        arrive(line3, lsem.at[4])
        rows = lax.broadcasted_iota(jnp.int32, (16, HEAD), 0)
        live2 = jnp.where(line2[...] >= 0, 0.0, NEG)
        live3 = jnp.where(line3[...] >= 0, 0.0, NEG)
        live3 = jnp.concatenate([live3, live3], axis=1)
        bias[...] = jnp.where(rows == 0, live2, jnp.where(rows == 1, live3, 0.0)).astype(BF16)

    def keys_send():
        slot = kv.at[y, zpar]
        sem = kvin.at[zpar]

        def each(parts):
            for hh in (0, 1):
                here = (zhalf == c) & (zpar == hh)
                away = jnp.logical_not(here)
                to = device(y, 2 * c + hh, zh, x, zhalf)
                for src, dst in parts(pl.ds(hh * HEAD, HEAD)):
                    keep(src, dst, sem, here)
                    send(src, dst, sem, to, away)

        each(lambda cols: (
            (k2.at[:, cols], slot.at[0:R2]),
            (k3.at[:, cols], slot.at[R2:RT]),
            (v2.at[:, cols], slot.at[RT:RT + R2]),
            (v3.at[:, cols], slot.at[RT + R2:GRAD]),
        ))
        make_bias()
        each(lambda cols: ((bias, slot.at[GRAD:SLOT]),))

    def cot_near():
        for dx in (1, 3, 2):
            to = device(y, z, zh, lax.rem(x + dx, 4), c)
            send(cot2, mine2, cot_x.at[0, 0, x], to)
            send(cot3, mine3, cot_x.at[1, 0, x], to)
        send(cot2, mine2, cot_s.at[0, zh, x], sibling)
        send(cot3, mine3, cot_s.at[1, zh, x], sibling)

    def cot_arrive(zz, xx, kind):
        for depth, ref in enumerate((ct2_at(zz, xx, c), ct3.at[zz, xx, c])):
            arrive(ref, cot_x.at[depth, kind, xx])
            send(ref, ref, cot_s.at[depth, zz, xx], sibling)

    def rows2(zz):
        return pl.ds(pl.multiple_of(zz * R2, R2), R2)

    def rows3(zz):
        return pl.ds(pl.multiple_of(zz * R3, R3), R3)

    def to_workers(hh, parts, places, sems):
        here = (zhalf == c) & (zpar == hh)
        away = jnp.logical_not(here)
        to = device(y, 2 * c + hh, zh, x, zhalf)
        for depth, (src, dst) in enumerate(zip(parts, places(z))):
            keep(src, dst, sems.at[z, depth], here)
            send(src, dst, sems.at[z, depth], to, away)

    def hand_on(places, sems):
        for k in (0, 1):
            for depth, ref in enumerate(places(2 * c + k)):
                sem = sems.at[2 * c + k, depth]
                arrive(ref, sem)
                send(ref, ref, sem, sibling)

    def handed(places, sems):
        for k in (0, 1):
            for depth, ref in enumerate(places(2 * (1 - c) + k)):
                arrive(ref, sems.at[2 * (1 - c) + k, depth])

    def query_places(zz):
        return qb2.at[rows2(zz)], qb3.at[rows3(zz)]

    def outer_places(zz):
        return ob2.at[:, rows2(zz)], ob3.at[rows3(zz)]

    def queries_send():
        for hh in (0, 1):
            cols = pl.ds(hh * HEAD, HEAD)
            to_workers(hh, (q2.at[:, cols], q3.at[:, cols]), query_places, qin)

    ring_to = (device(y_up, z, zh, x, c), device(y_down, z, zh, x, c))

    def origin(direction, step):
        return lax.rem(y + (8 - step if direction == 0 else step), 8)

    ring_sent = []

    def ring_send(direction, step, sub, at):
        slot = kv.at[at, sub]
        copy = pltpu.make_async_remote_copy(
            src_ref=slot, dst_ref=slot, send_sem=ring_s.at[direction, step, sub], recv_sem=ring.at[direction, step, sub],
            device_id=ring_to[direction], device_id_type=MESH,
        )
        copy.start()
        ring_sent.append(copy)

    def ring_step(step):
        for sub in (0, 1):
            for direction in (0, 1):
                if step == 4 and sub != direction:
                    continue
                at = origin(direction, step)
                arrive(kv.at[at, sub], ring.at[direction, step - 1, sub])
                if step < 3 or (step == 3 and sub == direction):
                    ring_send(direction, step, sub, at)

    row2 = pl.ds(0, 512)
    row3 = pl.ds(512, 256)

    def both(at, rows):
        return jnp.concatenate([kv[at, 0, rows], kv[at, 1, rows]], axis=0)

    def early_part(at, rows_k, rows_v, queries, column, row, store, acc, first):
        scores = dot_nn(both(at, rows_k), queries[...]) * SCALE_TWO + column
        if first is not None:
            key_slot = lax.broadcasted_iota(jnp.int32, scores.shape, 0) + first
            query_slot = lax.broadcasted_iota(jnp.int32, scores.shape, 1)
            scores = jnp.where(key_slot <= query_slot, scores, NEG)
        store[at] = scores
        before = stat[0:1, row]
        now = jnp.maximum(before, jnp.max(scores, axis=0, keepdims=True))
        weights = jnp.exp2(scores - now)
        fade = jnp.exp2(before - now)
        stat[0:1, row] = now
        stat[1:2, row] = stat[1:2, row] * fade + jnp.sum(weights, axis=0, keepdims=True)
        acc[...] = acc[...] * fade + dot_tn(both(at, rows_v), weights.astype(BF16))

    def early_now(at, own):
        lines = [kv[at, sub, GRAD:SLOT].astype(F32) for sub in (0, 1)]
        turned = jnp.concatenate(lines + [jnp.zeros((HEAD - 32, HEAD), F32)], axis=0).T
        column2 = jnp.concatenate([turned[:, 0:1], turned[:, 16:17]], axis=0)
        column3 = jnp.concatenate([turned[0:R3, 1:2], turned[0:R3, 17:18]], axis=0)
        early_part(at, pl.ds(0, R2), pl.ds(RT, R2), qt2, column2, row2, st2, acc2, 2 * R2 * c if own else None)
        early_part(at, pl.ds(R2, R3), pl.ds(RT + R2, R3), qt3, column3, row3, st3, acc3, 2 * R3 * c if own else None)

    def early_step(step):
        if step == 0:
            early_now(y, True)
            return

        @pl.loop(0, 1 if step == 4 else 2)
        def _(forward):
            at = lax.rem(y + 8 + (2 * forward - 1) * step, 8)

            @pl.when(at < y)
            def _():
                early_now(at, False)

    def own_keys():
        arrive(kv.at[y, 0], kvin.at[0])
        arrive(kv.at[y, 1], kvin.at[1])
        for sub in (0, 1):
            for direction in (0, 1):
                ring_send(direction, 0, sub, y)

    def near_shards():
        for dx in (1, 3, 2):
            cot_arrive(zh, lax.rem(x + dx, 4), 0)

    def queries_over():
        hand_on(query_places, qin)

    def queries_here():
        handed(query_places, qin)
        qt2[...] = qb2[...].T
        qt3[...] = qb3[...].T

    def far_shard(depth):
        other = (ct2_at(1 - zh, x, c), ct3.at[1 - zh, x, c])[depth]
        arrive(other, cot_z.at[depth])
        for dx in (1, 3, 2):
            to = device(y, z, zh, lax.rem(x + dx, 4), c)
            send(other, other, cot_x.at[depth, 1, x], to)
        send(other, other, cot_s.at[depth, 1 - zh, x], sibling)

    def far_near_shards():
        for dx in (1, 3, 2):
            cot_arrive(1 - zh, lax.rem(x + dx, 4), 1)

    def project(zz):
        totals = [outer2[...], outer3[...]]
        for xx in range(4):
            part = wv[:, pl.ds(pl.multiple_of((zz * 4 + xx) * 2 * FEAT, HEAD), 2 * FEAT)]
            features = jnp.concatenate([ct3[zz, xx, 0], ct3[zz, xx, 1]], axis=1)
            totals[0] += dot_nn(part, ct2[zz, xx])
            totals[1] += dot_nt(part, features)
        outer2[...], outer3[...] = totals

    def sibling_shards(zz):
        for xx in range(4):
            arrive(ct2_at(zz, xx, 1 - c), cot_s.at[0, zz, xx])
            arrive(ct3.at[zz, xx, 1 - c], cot_s.at[1, zz, xx])

    def near_project():
        arrive(mine2, lsem.at[0])
        arrive(mine3, lsem.at[1])
        arrive(wv, lsem.at[2])
        sibling_shards(zh)
        project(zh)

    def far_project():
        sibling_shards(1 - zh)
        project(1 - zh)

    def outer_send():
        lines = bias[...].astype(F32)
        dead = jnp.concatenate([lines, jnp.zeros((HEAD - 16, HEAD), F32)], axis=0).T[0:R3, 1:2]
        part2 = jnp.where(lines[0:1] < 0.0, 0.0, outer2[...]).astype(BF16)
        part3 = jnp.where(dead < 0.0, 0.0, outer3[...].T).astype(BF16)
        for hh in (0, 1):
            ost2[hh] = part2[hh * HEAD:(hh + 1) * HEAD]
            ost3[hh] = part3[:, hh * HEAD:(hh + 1) * HEAD]
            to_workers(hh, (ost2.at[hh], ost3.at[hh]), outer_places, oin)

    def outer_here():
        hand_on(outer_places, oin)
        handed(outer_places, oin)

    keys_send()
    cot_far()
    cot_near()
    clear()
    own_keys()
    near_shards()
    queries_send()
    ring_step(1)
    far_shard(0)
    far_shard(1)
    queries_over()
    queries_here()
    early_step(0)
    ring_step(2)
    near_project()
    early_step(1)
    far_near_shards()
    ring_step(3)
    far_project()
    outer_send()
    early_step(2)
    ring_step(4)
    early_step(3)
    early_step(4)
    outer_here()

    stat_out[...] = stat[...]
    stat_out[2:3, row2] = jnp.sum(ob2[...].astype(F32) * acc2[...], axis=0, keepdims=True)
    stat_out[2:3, row3] = jnp.sum(ob3[...].astype(F32).T * acc3[...], axis=0, keepdims=True)
    send(stat_out, stat_in, xsem.at[0], sibling)
    arrive(stat_in, xsem.at[0])
    top = jnp.maximum(stat_out[0:1], stat_in[0:1])
    own_part, other_part = jnp.exp2(stat_out[0:1] - top), jnp.exp2(stat_in[0:1] - top)
    total = stat_out[1:2] * own_part + stat_in[1:2] * other_part
    stat[3:4] = top + jnp.log2(total)
    stat[4:5] = (stat_out[2:3] * own_part + stat_in[2:3] * other_part) / total

    def late_part(at, rows_k, rows_v, queries, outers, row, store, dqt, by_rows, by_columns):
        probability = jnp.exp2(store[at] - stat[3:4, row])
        grad_probs = by_rows(both(at, rows_v), outers[...])
        grad_low = (probability * (grad_probs - stat[4:5, row])).astype(BF16)
        keys = dot_nn(grad_low, queries[...]) * SCALE
        values = by_columns(probability.astype(BF16), outers[...])
        count = keys.shape[0] // 2
        for sub in (0, 1):
            tmp[sub, rows_k] = keys[sub * count:(sub + 1) * count]
            tmp[sub, rows_v] = values[sub * count:(sub + 1) * count]
        half = grad_low.shape[1] // 2
        for h in (0, 1):
            dqt[h] += dot_tn(both(at, rows_k), grad_low[:, h * half:(h + 1) * half])

    def late_now(at):
        late_part(at, pl.ds(0, R2), pl.ds(RT, R2), qb2, ob2, row2, st2, dqt2, dot_nn, dot_nt)
        late_part(at, pl.ds(R2, R3), pl.ds(RT + R2, R3), qb3, ob3, row3, st3, dqt3, dot_nt, dot_nn)

    def late(at):
        @pl.when(at < y)
        def _():
            late_now(at)

        @pl.when(at > y)
        def _():
            tmp[...] = jnp.zeros_like(tmp)

    def red_copy(direction, step, sub):
        return pltpu.make_async_remote_copy(
            src_ref=sb.at[direction, step, sub], dst_ref=rb.at[direction, step, sub],
            send_sem=red_s.at[direction, step, sub], recv_sem=red.at[direction, step, sub],
            device_id=device(lax.rem(y + 1 + 6 * direction, 8), z, zh, x, c), device_id_type=MESH,
        )

    late(lax.rem(y + 4, 8))
    for sub in (0, 1):
        sb[sub, 0, sub] = tmp[sub].astype(BF16)
        red_copy(sub, 0, sub).start()
    for step in (1, 2, 3):

        @pl.loop(0, 2)
        def _(direction):
            late(lax.rem(y + (4 - step) + direction * 2 * (4 + step), 8))
            for sub in (0, 1):

                def add():
                    arrive(rb.at[direction, step - 1, sub], red.at[direction, step - 1, sub])
                    tmp[sub] += rb[direction, step - 1, sub].astype(F32)

                if step == 1:
                    pl.when(direction == sub)(add)
                else:
                    add()
                sb[direction, step, sub] = tmp[sub].astype(BF16)
                red_copy(direction, step, sub).start()

    late_now(y)

    dqx_out[:, 0:256] = dqt2[1 - c].astype(BF16)
    dqx_out[:, 256:384] = dqt3[1 - c].astype(BF16)
    send(dqx_out, dqx_in, xsem.at[1], sibling)
    arrive(dqx_in, xsem.at[1])
    query_two = (dqt2[c] + dqx_in[:, 0:256].astype(F32)) * SCALE
    query_three = (dqt3[c] + dqx_in[:, 256:384].astype(F32)) * SCALE
    rows_two, rows_three = query_two.T.astype(BF16), query_three.T.astype(BF16)

    def to_source(sub, src, dst, sems):
        here = (z == 2 * c + sub)
        to = device(y, 2 * c + sub, zh, x, zhalf)
        away = jnp.logical_not(here & (zhalf == c))
        keep(src, dst.at[zpar], sems.at[zpar], jnp.logical_not(away))
        send(src, dst.at[zpar], sems.at[zpar], to, away)

    for sub in (0, 1):
        dq_out[sub, 0:R2] = rows_two[sub * R2:(sub + 1) * R2]
        dq_out[sub, R2:RT] = rows_three[sub * R3:(sub + 1) * R3]
        to_source(sub, dq_out.at[sub], dq_in, dqsem)

    for sub in (0, 1):
        value = tmp[sub]
        for direction in (0, 1):
            arrive(rb.at[direction, 3, sub], red.at[direction, 3, sub])
            value = value + rb[direction, 3, sub].astype(F32)
        back_out[sub] = value.astype(BF16)
        to_source(sub, back_out.at[sub], back_in, backsem)

    for hh in (0, 1):
        arrive(dq_in.at[hh], dqsem.at[hh])
    dq_got[...] = dq_in[...]
    for hh in (0, 1):
        arrive(back_in.at[hh], backsem.at[hh])
    back_got[...] = back_in[...]

    for copy, when in sent:
        if when is None:
            copy.wait_send()
        else:
            pl.when(when)(copy.wait_send)
    for copy in ring_sent:
        copy.wait_send()
    for step in range(4):
        for sub in (0, 1):
            for direction in (0, 1):
                if step > 0 or sub == direction:
                    red_copy(direction, step, sub).wait_send()


def lay_out(dq_got, back_got, dq2, dk2, dv2, dq3, dk3, dv3, sem):
    copies = []
    for hh in (0, 1):
        cols = pl.ds(hh * HEAD, HEAD)
        parts = (
            (back_got.at[hh, 0:R2], dk2),
            (back_got.at[hh, RT:RT + R2], dv2),
            (dq_got.at[hh, 0:R2], dq2),
            (back_got.at[hh, R2:RT], dk3),
            (back_got.at[hh, RT + R2:GRAD], dv3),
            (dq_got.at[hh, R2:RT], dq3),
        )
        for src, dst in parts:
            copies.append(pltpu.make_async_copy(src, dst.at[:, cols], sem.at[len(copies)]))
    for copy in copies:
        copy.start()
    for copy in copies:
        copy.wait()


def on_device(q2, k2, v2, cot2, kept2, q3, k3, v3, cot3, kept3, weight):
    hbm = pl.BlockSpec(memory_space=pltpu.HBM)
    vmem = pl.BlockSpec(memory_space=pltpu.VMEM)
    dma = pltpu.SemaphoreType.DMA
    line2 = kept2.reshape(1, R2)
    line3 = kept3.reshape(1, R3)
    got = pl.pallas_call(
        body,
        out_shape=(
            jax.ShapeDtypeStruct((2, RT, HEAD), BF16),
            jax.ShapeDtypeStruct((2, GRAD, HEAD), BF16),
        ),
        in_specs=[hbm] * 11,
        out_specs=(vmem,) * 2,
        scratch_shapes=[
            pltpu.VMEM((2, 4, 2 * FEAT, R2), BF16),
            pltpu.VMEM((2, 4, 2, R3, FEAT), BF16),
            pltpu.VMEM((1, R2), jnp.int32),
            pltpu.VMEM((1, R3), jnp.int32),
            pltpu.VMEM((2 * HEAD, 16 * FEAT), BF16),
            pltpu.VMEM((8, 2, SLOT, HEAD), BF16),
            pltpu.VMEM((512, HEAD), BF16),
            pltpu.VMEM((256, HEAD), BF16),
            pltpu.VMEM((HEAD, 512), BF16),
            pltpu.VMEM((HEAD, 256), BF16),
            pltpu.VMEM((HEAD, 512), BF16),
            pltpu.VMEM((256, HEAD), BF16),
            pltpu.VMEM((16, HEAD), BF16),
            pltpu.VMEM((2 * HEAD, R2), F32),
            pltpu.VMEM((2 * HEAD, R3), F32),
            pltpu.VMEM((2, HEAD, R2), BF16),
            pltpu.VMEM((2, R3, HEAD), BF16),
            pltpu.VMEM((HEAD, 512), F32),
            pltpu.VMEM((HEAD, 256), F32),
            pltpu.VMEM((8, 2 * R2, 512), F32),
            pltpu.VMEM((8, 2 * R3, 256), F32),
            pltpu.VMEM((8, 768), F32),
            pltpu.VMEM((8, 768), F32),
            pltpu.VMEM((8, 768), F32),
            pltpu.VMEM((2, 4, 2, GRAD, HEAD), BF16),
            pltpu.VMEM((2, 4, 2, GRAD, HEAD), BF16),
            pltpu.VMEM((2, GRAD, HEAD), F32),
            pltpu.VMEM((2, HEAD, 256), F32),
            pltpu.VMEM((2, HEAD, 128), F32),
            pltpu.VMEM((HEAD, 384), BF16),
            pltpu.VMEM((HEAD, 384), BF16),
            pltpu.VMEM((2, RT, HEAD), BF16),
            pltpu.VMEM((2, RT, HEAD), BF16),
            pltpu.VMEM((2, GRAD, HEAD), BF16),
            pltpu.VMEM((2, GRAD, HEAD), BF16),
            dma((80,)),
            dma((5,)),
            dma((2,)),
            dma((2, 2, 4)),
            dma((2, 2, 4)),
            dma((2,)),
            dma((4, 2)),
            dma((4, 2)),
            dma((2, 4, 2)),
            dma((2, 4, 2)),
            dma((2, 4, 2)),
            dma((2, 4, 2)),
            dma((2,)),
            dma((2,)),
            dma((2,)),
        ],
        compiler_params=pltpu.CompilerParams(
            collective_id=0, has_side_effects=True, vmem_limit_bytes=64 * 1024 * 1024
        ),
        name="attention_backward",
    )(line2, line3, q2, k2, v2, cot2.T, q3, k3, v3, cot3, weight)
    wide = jax.ShapeDtypeStruct((R2, 2 * HEAD), BF16)
    narrow = jax.ShapeDtypeStruct((R3, 2 * HEAD), BF16)
    return pl.pallas_call(
        lay_out,
        out_shape=(wide, wide, wide, narrow, narrow, narrow),
        in_specs=[vmem] * 2,
        out_specs=(hbm,) * 6,
        scratch_shapes=[dma((12,))],
        name="lay_out",
    )(*got)


def solution(mesh):
    shard = P("seq", "tp")
    in_specs = (shard, shard, shard, shard, P("seq"), shard, shard, shard, shard, P("seq"), P("tp", None))
    return jax.shard_map(on_device, mesh=mesh, in_specs=in_specs, out_specs=(shard,) * 6, check_vma=False)
```

time: 94.7 us -> 80.4 us (0.85)
  local copies, waits for them, and re-layouts: 13.4 us -> 0 us
    unnamed x25 -> x0, local copies, waits for them, and re-layouts: 12.7 us -> none
    pallas_call x1 -> x2, Pallas kernels: 80.1 us -> 79.6 us  [the longest x1 77.8 us: on_device(): pl.pallas_call(body, out_shape=(jax.ShapeDtypeStruct((2, RT, HEAD), BF16)...]
where the time goes in v2:
time: 80.4 us; the launch traced here: 80.2 us
  Pallas kernels  79.6 us (99%)
    pallas_call x1, Pallas kernels, on_device(): pl.pallas_call(body, out_shape=(jax.ShapeDtypeStruct((2, RT, HEAD), BF16)...  77.8 us
    pallas_call x1, Pallas kernels, on_device(): pl.pallas_call(lay_out, out_shape=(wide, wide, wide, narrow, narrow, narr...  1.78 us

profile of v2, /device:TPU:1, one launch (start us, length us, event | category | flops | bytes accessed | tf_op | source)
XLA Modules:
  0.0 80.2 jit_solution(5521558048949677898)
XLA Ops:
  0.6 77.8 %attention_backward.1 = (bf16[2,192,128]{2,1,0:T(8,128)(2,1)}, bf16[2,384,128]{2,1,0:T(8,128)(2,1)}) custom-call(s32[1,128]{1,0:T(1,128)} %bitcast.4, s32[1,64]{1,0:T(1,128)} %bitcast.5, bf16[128,256]{1,0:T(8,128)(2,1)} %q2.1, bf16[128,256]{1,0:T(8,128)(2,1)} %k2.1, bf16[128,256]{1,0:T(8,128)(2,1)} %v2.1, bf16[320,128]{1,0:T(8,128)(2,1)} %bitcast.3, ...), custom_call_target="tpu_custom_call" | custom-call | tf_op jit(solution)/shard_map/attention_backward/pallas_call | solution.py:496
  78.4 1.8 %lay_out.1 = (bf16[128,256]{1,0:T(8,128)(2,1)}, bf16[128,256]{1,0:T(8,128)(2,1)}, bf16[128,256]{1,0:T(8,128)(2,1)}, bf16[64,256]{1,0:T(8,128)(2,1)}, bf16[64,256]{1,0:T(8,128)(2,1)}, /*index=5*/bf16[64,256]{1,0:T(8,128)(2,1)}) custom-call(bf16[2,192,128]{2,1,0:T(8,128)(2,1)} %get-tuple-element.8.dq_got, bf16[2,384,128]{2,1,0:T(8,128)(2,1)} %get-tuple-element.9.back_got), custom_call_target="tpu_custom_call" | custom-call | tf_op jit(solution)/shard_map/lay_out/pallas_call | solution.py:563

commit v3 on v2

--- a/solution.py
+++ b/solution.py
@@ -319,8 +319,10 @@
             ost3[hh] = part3[:, hh * HEAD:(hh + 1) * HEAD]
             to_workers(hh, (ost2.at[hh], ost3.at[hh]), outer_places, oin)
 
+    def outer_over():
+        hand_on(outer_places, oin)
+
     def outer_here():
-        hand_on(outer_places, oin)
         handed(outer_places, oin)
 
     keys_send()
@@ -344,8 +346,9 @@
     far_project()
     outer_send()
     early_step(2)
+    early_step(3)
     ring_step(4)
-    early_step(3)
+    outer_over()
     early_step(4)
     outer_here()
 
@@ -360,7 +363,7 @@
     stat[3:4] = top + jnp.log2(total)
     stat[4:5] = (stat_out[2:3] * own_part + stat_in[2:3] * other_part) / total
 
-    def late_part(at, rows_k, rows_v, queries, outers, row, store, dqt, by_rows, by_columns):
+    def late_part(at, side, rows_k, rows_v, queries, outers, row, store, dqt, by_rows, by_columns):
         probability = jnp.exp2(store[at] - stat[3:4, row])
         grad_probs = by_rows(both(at, rows_v), outers[...])
         grad_low = (probability * (grad_probs - stat[4:5, row])).astype(BF16)
@@ -368,55 +371,61 @@
         values = by_columns(probability.astype(BF16), outers[...])
         count = keys.shape[0] // 2
         for sub in (0, 1):
-            tmp[sub, rows_k] = keys[sub * count:(sub + 1) * count]
-            tmp[sub, rows_v] = values[sub * count:(sub + 1) * count]
+            tmp[side, sub, rows_k] = keys[sub * count:(sub + 1) * count]
+            tmp[side, sub, rows_v] = values[sub * count:(sub + 1) * count]
         half = grad_low.shape[1] // 2
         for h in (0, 1):
             dqt[h] += dot_tn(both(at, rows_k), grad_low[:, h * half:(h + 1) * half])
 
-    def late_now(at):
-        late_part(at, pl.ds(0, R2), pl.ds(RT, R2), qb2, ob2, row2, st2, dqt2, dot_nn, dot_nt)
-        late_part(at, pl.ds(R2, R3), pl.ds(RT + R2, R3), qb3, ob3, row3, st3, dqt3, dot_nt, dot_nn)
-
-    def late(at):
+    def late_now(at, side):
+        late_part(at, side, pl.ds(0, R2), pl.ds(RT, R2), qb2, ob2, row2, st2, dqt2, dot_nn, dot_nt)
+        late_part(at, side, pl.ds(R2, R3), pl.ds(RT + R2, R3), qb3, ob3, row3, st3, dqt3, dot_nt, dot_nn)
+
+    def late(at, side):
         @pl.when(at < y)
         def _():
-            late_now(at)
+            late_now(at, side)
 
         @pl.when(at > y)
         def _():
-            tmp[...] = jnp.zeros_like(tmp)
-
-    def red_copy(direction, step, sub):
+            tmp[side] = jnp.zeros((2, GRAD, HEAD), F32)
+
+    def red_copy(direction, step, sub, part):
+        rows = pl.ds(part * RT, RT)
         return pltpu.make_async_remote_copy(
-            src_ref=sb.at[direction, step, sub], dst_ref=rb.at[direction, step, sub],
-            send_sem=red_s.at[direction, step, sub], recv_sem=red.at[direction, step, sub],
-            device_id=device(lax.rem(y + 1 + 6 * direction, 8), z, zh, x, c), device_id_type=MESH,
+            src_ref=sb.at[direction, step, sub, rows], dst_ref=rb.at[direction, step, sub, rows],
+            send_sem=red_s.at[direction, step, sub, part], recv_sem=red.at[direction, step, sub, part],
+            device_id=ring_to[direction], device_id_type=MESH,
         )
 
-    late(lax.rem(y + 4, 8))
+    def red_here(direction, step, sub, part):
+        rows = pl.ds(part * RT, RT)
+        arrive(rb.at[direction, step, sub, rows], red.at[direction, step, sub, part])
+        return rb[direction, step, sub, rows].astype(F32)
+
+    def red_send(direction, step, sub, add, side):
+        for part in (0, 1):
+            rows = pl.ds(part * RT, RT)
+            value = tmp[side, sub, rows]
+            if add:
+                value = value + red_here(direction, step - 1, sub, part)
+            sb[direction, step, sub, rows] = value.astype(BF16)
+            red_copy(direction, step, sub, part).start()
+
+    red_order = ((0, 1), (1, 0), (0, 0), (1, 1))
+    late(lax.rem(y + 4, 8), 0)
     for sub in (0, 1):
-        sb[sub, 0, sub] = tmp[sub].astype(BF16)
-        red_copy(sub, 0, sub).start()
+        red_send(sub, 0, sub, False, 0)
     for step in (1, 2, 3):
 
         @pl.loop(0, 2)
-        def _(direction):
-            late(lax.rem(y + (4 - step) + direction * 2 * (4 + step), 8))
-            for sub in (0, 1):
-
-                def add():
-                    arrive(rb.at[direction, step - 1, sub], red.at[direction, step - 1, sub])
-                    tmp[sub] += rb[direction, step - 1, sub].astype(F32)
-
-                if step == 1:
-                    pl.when(direction == sub)(add)
-                else:
-                    add()
-                sb[direction, step, sub] = tmp[sub].astype(BF16)
-                red_copy(direction, step, sub).start()
-
-    late_now(y)
+        def _(side):
+            late(lax.rem(y + (4 - step) + side * 2 * (4 + step), 8), side)
+
+        for direction, sub in red_order:
+            red_send(direction, step, sub, step > 1 or direction == sub, direction)
+
+    late_now(y, 0)
 
     dqx_out[:, 0:256] = dqt2[1 - c].astype(BF16)
     dqx_out[:, 256:384] = dqt3[1 - c].astype(BF16)
@@ -426,31 +435,32 @@
     query_three = (dqt3[c] + dqx_in[:, 256:384].astype(F32)) * SCALE
     rows_two, rows_three = query_two.T.astype(BF16), query_three.T.astype(BF16)
 
-    def to_source(sub, src, dst, sems):
-        here = (z == 2 * c + sub)
+    def to_source(src, dst, sem, sub):
         to = device(y, 2 * c + sub, zh, x, zhalf)
-        away = jnp.logical_not(here & (zhalf == c))
-        keep(src, dst.at[zpar], sems.at[zpar], jnp.logical_not(away))
-        send(src, dst.at[zpar], sems.at[zpar], to, away)
+        here = (z == 2 * c + sub) & (zhalf == c)
+        keep(src, dst, sem, here)
+        send(src, dst, sem, to, jnp.logical_not(here))
 
     for sub in (0, 1):
         dq_out[sub, 0:R2] = rows_two[sub * R2:(sub + 1) * R2]
         dq_out[sub, R2:RT] = rows_three[sub * R3:(sub + 1) * R3]
-        to_source(sub, dq_out.at[sub], dq_in, dqsem)
-
-    for sub in (0, 1):
-        value = tmp[sub]
-        for direction in (0, 1):
-            arrive(rb.at[direction, 3, sub], red.at[direction, 3, sub])
-            value = value + rb[direction, 3, sub].astype(F32)
-        back_out[sub] = value.astype(BF16)
-        to_source(sub, back_out.at[sub], back_in, backsem)
+        to_source(dq_out.at[sub], dq_in.at[zpar], dqsem.at[zpar], sub)
+
+    for part in (0, 1):
+        rows = pl.ds(part * RT, RT)
+        for sub in (0, 1):
+            value = tmp[0, sub, rows]
+            for direction in (sub, 1 - sub):
+                value = value + red_here(direction, 3, sub, part)
+            back_out[sub, rows] = value.astype(BF16)
+            to_source(back_out.at[sub, rows], back_in.at[zpar, rows], backsem.at[zpar, part], sub)
 
     for hh in (0, 1):
         arrive(dq_in.at[hh], dqsem.at[hh])
     dq_got[...] = dq_in[...]
     for hh in (0, 1):
-        arrive(back_in.at[hh], backsem.at[hh])
+        for part in (0, 1):
+            arrive(back_in.at[hh, pl.ds(part * RT, RT)], backsem.at[hh, part])
     back_got[...] = back_in[...]
 
     for copy, when in sent:
@@ -464,7 +474,8 @@
         for sub in (0, 1):
             for direction in (0, 1):
                 if step > 0 or sub == direction:
-                    red_copy(direction, step, sub).wait_send()
+                    for part in (0, 1):
+                        red_copy(direction, step, sub, part).wait_send()
 
 
 def lay_out(dq_got, back_got, dq2, dk2, dv2, dq3, dk3, dv3, sem):
@@ -528,7 +539,7 @@
             pltpu.VMEM((8, 768), F32),
             pltpu.VMEM((2, 4, 2, GRAD, HEAD), BF16),
             pltpu.VMEM((2, 4, 2, GRAD, HEAD), BF16),
-            pltpu.VMEM((2, GRAD, HEAD), F32),
+            pltpu.VMEM((2, 2, GRAD, HEAD), F32),
             pltpu.VMEM((2, HEAD, 256), F32),
             pltpu.VMEM((2, HEAD, 128), F32),
             pltpu.VMEM((HEAD, 384), BF16),
@@ -546,11 +557,11 @@
             dma((4, 2)),
             dma((4, 2)),
             dma((2, 4, 2)),
+            dma((2, 4, 2, 2)),
             dma((2, 4, 2)),
-            dma((2, 4, 2)),
-            dma((2, 4, 2)),
+            dma((2, 4, 2, 2)),
             dma((2,)),
-            dma((2,)),
+            dma((2, 2)),
             dma((2,)),
         ],
         compiler_params=pltpu.CompilerParams(

time: 80.4 us -> 76.2 us (0.948)
  Pallas kernels: 79.6 us -> 75.4 us
    pallas_call x1, Pallas kernels: 77.8 us -> 73.6 us  [on_device(): pl.pallas_call(body, out_shape=(jax.ShapeDtypeStruct((2, RT, HEAD), BF16)...]
where the time goes in v3:
time: 76.2 us; the launch traced here: 76 us
  Pallas kernels  75.4 us (99%)
    pallas_call x1, Pallas kernels, on_device(): pl.pallas_call(body, out_shape=(jax.ShapeDtypeStruct((2, RT, HEAD), BF16)...  73.6 us
    pallas_call x1, Pallas kernels, on_device(): pl.pallas_call(lay_out, out_shape=(wide, wide, wide, narrow, narrow, narr...  1.78 us

profile of v3, /device:TPU:1, one launch (start us, length us, event | category | flops | bytes accessed | tf_op | source)
XLA Modules:
  0.0 76.0 jit_solution(8812688271790872190)
XLA Ops:
  0.6 73.6 %attention_backward.1 = (bf16[2,192,128]{2,1,0:T(8,128)(2,1)}, bf16[2,384,128]{2,1,0:T(8,128)(2,1)}) custom-call(s32[1,128]{1,0:T(1,128)} %bitcast.4, s32[1,64]{1,0:T(1,128)} %bitcast.5, bf16[128,256]{1,0:T(8,128)(2,1)} %q2.1, bf16[128,256]{1,0:T(8,128)(2,1)} %k2.1, bf16[128,256]{1,0:T(8,128)(2,1)} %v2.1, bf16[320,128]{1,0:T(8,128)(2,1)} %bitcast.3, ...), custom_call_target="tpu_custom_call" | custom-call | tf_op jit(solution)/shard_map/attention_backward/pallas_call | solution.py:507
  74.2 1.8 %lay_out.1 = (bf16[128,256]{1,0:T(8,128)(2,1)}, bf16[128,256]{1,0:T(8,128)(2,1)}, bf16[128,256]{1,0:T(8,128)(2,1)}, bf16[64,256]{1,0:T(8,128)(2,1)}, bf16[64,256]{1,0:T(8,128)(2,1)}, /*index=5*/bf16[64,256]{1,0:T(8,128)(2,1)}) custom-call(bf16[2,192,128]{2,1,0:T(8,128)(2,1)} %get-tuple-element.8.dq_got, bf16[2,384,128]{2,1,0:T(8,128)(2,1)} %get-tuple-element.9.back_got), custom_call_target="tpu_custom_call" | custom-call | tf_op jit(solution)/shard_map/lay_out/pallas_call | solution.py:574

commit v4 on v3

--- a/solution.py
+++ b/solution.py
@@ -42,7 +42,7 @@
     dq_got, back_got,
     ct2, ct3, line2, line3, wv, kv, qb2, qb3, qt2, qt3, ob2, ob3, bias, outer2, outer3, ost2, ost3, acc2, acc3, st2, st3,
     stat, stat_out, stat_in, rb, sb, tmp, dqt2, dqt3, dqx_out, dqx_in, dq_out, dq_in, back_out, back_in,
-    ssem, lsem, cot_z, cot_x, cot_s, kvin, qin, oin, ring, red, ring_s, red_s, xsem, backsem, dqsem,
+    ssem, lsem, cot_z, cot_x, cot_s, kvin, qin, oin, ring, red, ring_s, red_s, xsem, backsem, dqsem, outsem,
 ):
     s, t = lax.axis_index("seq"), lax.axis_index("tp")
     y, z = lax.div(s, 4), lax.rem(s, 4)
@@ -455,13 +455,17 @@
             back_out[sub, rows] = value.astype(BF16)
             to_source(back_out.at[sub, rows], back_in.at[zpar, rows], backsem.at[zpar, part], sub)
 
-    for hh in (0, 1):
-        arrive(dq_in.at[hh], dqsem.at[hh])
-    dq_got[...] = dq_in[...]
-    for hh in (0, 1):
+    def results():
+        for hh in (0, 1):
+            yield dq_in.at[hh], dqsem.at[hh], dq_got.at[hh], outsem.at[hh]
         for part in (0, 1):
-            arrive(back_in.at[hh, pl.ds(part * RT, RT)], backsem.at[hh, part])
-    back_got[...] = back_in[...]
+            rows = pl.ds(part * RT, RT)
+            for hh in (0, 1):
+                yield back_in.at[hh, rows], backsem.at[hh, part], back_got.at[hh, rows], outsem.at[2 + 2 * part + hh]
+
+    for src, sem, dst, out_sem in results():
+        arrive(src, sem)
+        pltpu.make_async_copy(src, dst, out_sem).start()
 
     for copy, when in sent:
         if when is None:
@@ -476,6 +480,8 @@
                 if step > 0 or sub == direction:
                     for part in (0, 1):
                         red_copy(direction, step, sub, part).wait_send()
+    for src, _, dst, out_sem in results():
+        pltpu.make_async_copy(src, dst, out_sem).wait()
 
 
 def lay_out(dq_got, back_got, dq2, dk2, dv2, dq3, dk3, dv3, sem):
@@ -500,7 +506,6 @@
 
 def on_device(q2, k2, v2, cot2, kept2, q3, k3, v3, cot3, kept3, weight):
     hbm = pl.BlockSpec(memory_space=pltpu.HBM)
-    vmem = pl.BlockSpec(memory_space=pltpu.VMEM)
     dma = pltpu.SemaphoreType.DMA
     line2 = kept2.reshape(1, R2)
     line3 = kept3.reshape(1, R3)
@@ -511,7 +516,7 @@
             jax.ShapeDtypeStruct((2, GRAD, HEAD), BF16),
         ),
         in_specs=[hbm] * 11,
-        out_specs=(vmem,) * 2,
+        out_specs=(hbm,) * 2,
         scratch_shapes=[
             pltpu.VMEM((2, 4, 2 * FEAT, R2), BF16),
             pltpu.VMEM((2, 4, 2, R3, FEAT), BF16),
@@ -563,6 +568,7 @@
             dma((2,)),
             dma((2, 2)),
             dma((2,)),
+            dma((6,)),
         ],
         compiler_params=pltpu.CompilerParams(
             collective_id=0, has_side_effects=True, vmem_limit_bytes=64 * 1024 * 1024
@@ -574,7 +580,7 @@
     return pl.pallas_call(
         lay_out,
         out_shape=(wide, wide, wide, narrow, narrow, narrow),
-        in_specs=[vmem] * 2,
+        in_specs=[pl.BlockSpec(memory_space=pltpu.VMEM)] * 2,
         out_specs=(hbm,) * 6,
         scratch_shapes=[dma((12,))],
         name="lay_out",

time: 76.2 us -> 76 us (level)
  no operation moved by 1% of the time
where the time goes in v4:
time: 76 us; the launch traced here: 75.8 us
  Pallas kernels  75.2 us (99%)
    pallas_call x1, Pallas kernels, on_device(): pl.pallas_call(body, out_shape=(jax.ShapeDtypeStruct((2, RT, HEAD), BF16)...  73.4 us
    pallas_call x1, Pallas kernels, on_device(): pl.pallas_call(lay_out, out_shape=(wide, wide, wide, narrow, narrow, narr...  1.78 us

profile of v4, /device:TPU:1, one launch (start us, length us, event | category | flops | bytes accessed | tf_op | source)
XLA Modules:
  0.0 75.8 jit_solution(3798282425671300647)
XLA Ops:
  0.6 73.4 %attention_backward.1 = (bf16[2,192,128]{2,1,0:T(8,128)(2,1)}, bf16[2,384,128]{2,1,0:T(8,128)(2,1)}) custom-call(s32[1,128]{1,0:T(1,128)} %bitcast.4, s32[1,64]{1,0:T(1,128)} %bitcast.5, bf16[128,256]{1,0:T(8,128)(2,1)} %q2.1, bf16[128,256]{1,0:T(8,128)(2,1)} %k2.1, bf16[128,256]{1,0:T(8,128)(2,1)} %v2.1, bf16[320,128]{1,0:T(8,128)(2,1)} %bitcast.3, ...), custom_call_target="tpu_custom_call" | custom-call | tf_op jit(solution)/shard_map/attention_backward/pallas_call | solution.py:512
  74.0 1.8 %lay_out.1 = (bf16[128,256]{1,0:T(8,128)(2,1)}, bf16[128,256]{1,0:T(8,128)(2,1)}, bf16[128,256]{1,0:T(8,128)(2,1)}, bf16[64,256]{1,0:T(8,128)(2,1)}, bf16[64,256]{1,0:T(8,128)(2,1)}, /*index=5*/bf16[64,256]{1,0:T(8,128)(2,1)}) custom-call(bf16[2,192,128]{2,1,0:T(8,128)(2,1)} %get-tuple-element.8.dq_got, bf16[2,384,128]{2,1,0:T(8,128)(2,1)} %get-tuple-element.9.back_got), custom_call_target="tpu_custom_call" | custom-call | tf_op jit(solution)/shard_map/lay_out/pallas_call | solution.py:580
